TPU v7x, 32 devices: a whole 2x2x4 slice. The times are simulated.
32 devices in a mesh: section: 2 (over core), dp: 8 (over z, x), tensor: 2 (over y).
Axes of the slice: x: 2, y: 2, z: 4, core: 2. Of those that a mesh axis runs over, the one named last changes fastest.
Arguments:
- x_input: bfloat16 [2, 8192, 768], P(None, ('dp', 'tensor')), may hold values from -6 to 6
- teacher: float32 [2, 8192, 768], P(None, ('dp', 'tensor')), may hold values from -6 to 6
- segment_ids: int32 [2, 8, 1024], P(None, 'dp'), may hold values from 0 to 2, as said below
- valid_len: int32 [2, 8], replicated, may hold values from 256 to 1024
- norm_gain: bfloat16 [2, 768], P('section', 'dp'), may hold values from 0.5 to 1.5
- w_zx: bfloat16 [2, 768, 2, 1536], P('section', 'dp', None, 'tensor'), may hold values from -0.21875 to 0.21875
- w_bc: bfloat16 [2, 768, 256], P('section', 'dp'), may hold values from -0.21875 to 0.21875
- w_dt: bfloat16 [2, 768, 24], P('section', 'dp', 'tensor'), may hold values from -0.21875 to 0.21875
- conv_x: bfloat16 [2, 5, 1536], P('section', None, 'tensor'), may hold values from -3 to 3
- conv_bc: bfloat16 [2, 5, 256], P('section'), may hold values from -3 to 3
- dt_bias: float32 [2, 24], P('section'), may hold values from -4.5 to -1.5
- a_log: float32 [2, 24], P('section'), may hold values from -4 to 2.5
- d_skip: float32 [2, 24], P('section'), may hold values from 0.5 to 1.5
- gnorm_gain: bfloat16 [2, 1536], P('section', 'tensor'), may hold values from 0.5 to 1.5
- w_out: bfloat16 [2, 1536, 768], P('section', 'tensor', 'dp'), may hold values from -0.15625 to 0.15625
Outputs:
- layer_outputs: bfloat16 [2, 2, 8192, 768], P('section', None, ('dp', 'tensor'))
- boundary_grads: float32 [2, 2, 8192, 768], P('section', None, ('dp', 'tensor'))
- grad_norm_gain: float32 [2, 768], P('section', 'dp')
- grad_w_zx: float32 [2, 768, 2, 1536], P('section', 'dp', None, 'tensor')
- grad_w_bc: float32 [2, 768, 256], P('section', 'dp')
- grad_w_dt: float32 [2, 768, 24], P('section', 'dp', 'tensor')
- grad_conv_x: float32 [2, 5, 1536], P('section', None, 'tensor')
- grad_conv_bc: float32 [2, 5, 256], P('section')
- grad_dt_bias: float32 [2, 24], P('section', 'tensor')
- grad_a_log: float32 [2, 24], P('section', 'tensor')
- grad_d_skip: float32 [2, 24], P('section', 'tensor')
- grad_gnorm_gain: float32 [2, 1536], P('section', 'tensor')
- grad_w_out: float32 [2, 1536, 768], P('section', 'tensor', 'dp')
Inputs may be any that keep to these rules, and one draw needn't show every extreme that they name: `segment_ids`: within each sequence the ids start at 0 at the first token, never fall, and rise by at most one from a token to the next; the last document is cut at the sequence's end.
All inputs are finite; a program needn't handle non-finite values.
Results may differ from a plain program's by a relative error of at most 0.019.
Values may be sent and summed in bfloat16 or wider, within the bound.
No kernel may reach another device: no remote copies, remote signals or barrier semaphores. Data moves between devices by JAX's collectives and lax.ppermute only.
A program may use at most 256 MiB of HBM per device.

v0:
```python
import jax
import jax.numpy as jnp
from jax import lax
from jax.sharding import PartitionSpec as P

HEAD_DIM = 64
STATE = 128
SPAN = 256


epsilon = 1e-05


def passed_along(block, axis, distance):
    devices = range(lax.axis_size(axis))
    route = [(i - distance, i) for i in devices if i - distance in devices]
    return lax.ppermute(block, axis, route)


def causal_conv(signal, taps, segment):
    reach = taps.shape[0] - 1
    length = signal.shape[0]
    result = taps[reach] + taps[reach - 1] * signal
    for lag in range(1, reach):
        moved = jnp.pad(signal, ((lag, 0), (0, 0)))[:length]
        moved_segment = jnp.pad(segment, (lag, 0), constant_values=-1)[:length]
        same = (moved_segment == segment).astype(jnp.float32)
        result = result + taps[reach - 1 - lag] * moved * same[:, None]
    return result


def block_scan(values, b_rows, c_rows, steps_dt, rates, segment):
    length, heads, head_width = values.shape
    blocks = length // SPAN
    values = values.reshape(blocks, SPAN, heads, head_width)
    b_rows = b_rows.reshape(blocks, SPAN, -1)
    c_rows = c_rows.reshape(blocks, SPAN, -1)
    steps_dt = steps_dt.reshape(blocks, SPAN, heads)
    segment = segment.reshape(blocks, SPAN)
    log_decay = jnp.cumsum(-steps_dt * rates, axis=1)
    scaled = values * steps_dt[..., None]
    lower = jnp.arange(SPAN)[:, None] >= jnp.arange(SPAN)[None, :]
    linked = lower[None] & (segment[:, :, None] == segment[:, None, :])
    decay_heads = jnp.transpose(log_decay, (0, 2, 1))
    gaps = decay_heads[:, :, :, None] - decay_heads[:, :, None, :]
    keep = linked[:, None]
    factors = jnp.where(keep, jnp.exp(jnp.where(keep, gaps, 0.0)), 0.0)
    scores = jnp.einsum("cis,cjs->cij", c_rows, b_rows, precision=lax.Precision.HIGHEST)
    inside = jnp.einsum(
        "chij,cjhp->cihp", factors * scores[:, None], scaled, precision=lax.Precision.HIGHEST
    )
    same_end = (segment == segment[:, -1:]).astype(jnp.float32)
    tail = jnp.exp(log_decay[:, -1:, :] - log_decay) * same_end[:, :, None]
    states = jnp.einsum(
        "cjhp,cjs->chps", tail[..., None] * scaled, b_rows, precision=lax.Precision.HIGHEST
    )

    def carry_step(carried, item):
        state, previous = carried
        log_block, c_block, segment_block, new_state = item
        entry = jnp.exp(log_block) * (segment_block == previous).astype(jnp.float32)[:, None]
        across = (
            jnp.einsum("is,hps->ihp", c_block, state, precision=lax.Precision.HIGHEST)
            * entry[:, :, None]
        )
        through = jnp.exp(log_block[-1]) * (segment_block[-1] == previous).astype(jnp.float32)
        state = through[:, None, None] * state + new_state
        return ((state, segment_block[-1]), across)

    start_state = jnp.zeros((heads, head_width, b_rows.shape[-1]), jnp.float32)
    start_segment = jnp.array(-1, jnp.int32)
    _, across = lax.scan(
        carry_step, (start_state, start_segment), (log_decay, c_rows, segment, states)
    )
    return (inside + across).reshape(length, heads, head_width)


def prepare(projected, tail_rows, before, conv_values, conv_states, bias_steps, segment):
    inner_width = conv_values.shape[1]
    state_end = 2 * inner_width + 2 * STATE
    joined_segment = jnp.concatenate([before, segment])
    value_rows = jnp.concatenate(
        [tail_rows[:, :inner_width], projected[:, inner_width : 2 * inner_width]], axis=0
    )
    state_rows = jnp.concatenate(
        [tail_rows[:, inner_width:], projected[:, 2 * inner_width : state_end]], axis=0
    )
    values = jax.nn.silu(causal_conv(value_rows, conv_values, joined_segment))
    states_in = jax.nn.silu(causal_conv(state_rows, conv_states, joined_segment))
    steps_dt = jax.nn.softplus(projected[:, state_end:] + bias_steps)
    shaped = values.reshape(values.shape[0], steps_dt.shape[1], HEAD_DIM)
    return (
        projected[:, :inner_width],
        shaped,
        states_in[:, :STATE],
        states_in[:, STATE:],
        steps_dt,
    )


def core(prepared, log_rates, skip_gains, segment):
    gate_part, shaped, b_rows, c_rows, steps_dt = prepared
    rates = jnp.exp(log_rates)
    result = block_scan(shaped, b_rows, c_rows, steps_dt, rates, segment)
    result = result + skip_gains[:, None] * shaped
    return result.reshape(shaped.shape[0], -1) * jax.nn.silu(gate_part)


def stack_steps(items):
    return jax.tree.map(lambda *parts: jnp.stack(parts), items[0], *items[1:])


def body(
    x_input,
    teacher,
    segment_ids,
    valid_len,
    norm_gain,
    w_zx,
    w_bc,
    w_dt,
    conv_x,
    conv_bc,
    dt_bias,
    a_log,
    d_skip,
    gnorm_gain,
    w_out,
):
    micro = x_input.shape[0]
    local_rows = x_input.shape[1]
    width = x_input.shape[2]
    seq_length = segment_ids.shape[2]
    splits = lax.axis_size("tensor")
    tensor_index = lax.axis_index("tensor")
    section_index = lax.axis_index("section")
    section_first = section_index == 0
    row_start = tensor_index * local_rows
    positions = row_start + jnp.arange(local_rows)
    counted = jnp.sum(valid_len).astype(jnp.float32)
    loss_weight = micro * seq_length * lax.axis_size("dp") / counted
    lengths_all = lax.dynamic_index_in_dim(valid_len, lax.axis_index("dp"), 1, keepdims=False)
    segments_all = segment_ids[:, 0]
    heads_local = dt_bias.shape[1] // splits
    head_start = tensor_index * heads_local
    inner_local = gnorm_gain.shape[1]
    inner_total = inner_local * splits

    def fetch():
        gathered = (
            lax.all_gather(norm_gain, "dp", axis=1, tiled=True),
            lax.all_gather(w_zx, "dp", axis=1, tiled=True),
            lax.all_gather(w_bc, "dp", axis=1, tiled=True),
            lax.all_gather(w_dt, "dp", axis=1, tiled=True),
            lax.all_gather(w_out, "dp", axis=2, tiled=True),
        )
        gain = gathered[0][0].astype(jnp.float32)
        pair = gathered[1][0]
        state_cols = gathered[2][0]
        step_cols = gathered[3][0]
        out_rows = gathered[4][0]
        conv_values, gate_gain = (conv_x[0], gnorm_gain[0])
        bias_steps = lax.dynamic_slice_in_dim(dt_bias[0], head_start, heads_local)
        log_rates = lax.dynamic_slice_in_dim(a_log[0], head_start, heads_local)
        skip_gains = lax.dynamic_slice_in_dim(d_skip[0], head_start, heads_local)
        w_in = jnp.concatenate([pair[:, 0], pair[:, 1], state_cols, step_cols], axis=1)
        smalls = (
            conv_values.astype(jnp.float32),
            conv_bc[0].astype(jnp.float32),
            bias_steps,
            log_rates,
            skip_gains,
        )
        return (gain, w_in, out_rows, smalls, gate_gain.astype(jnp.float32))

    empty_tail = jnp.zeros((0, inner_local + 2 * STATE), jnp.float32)
    empty_before = jnp.zeros((0,), jnp.int32)

    def gather_rows(rows_here):
        return lax.all_gather(rows_here, "tensor", axis=0, tiled=True)

    def unit_total(values):
        return lax.psum(values, "tensor")

    def row_total(term):
        return lax.psum_scatter(
            term(jnp.int32(0), local_rows * lax.axis_size("tensor")).astype(jnp.bfloat16),
            "tensor",
            scatter_dimension=0,
            tiled=True,
        ).astype(jnp.float32)

    def mixed_rows(normed, segment_whole, weights, with_pull):
        gain, w_in, out_rows, smalls, gate_gain = weights
        gathered = gather_rows(normed)
        projected = jnp.dot(gathered, w_in, preferred_element_type=jnp.float32)

        def local_mixer(projected_in, conv_values, conv_states, bias_steps, log_rates, skip_gains):
            prepared = prepare(
                projected_in,
                empty_tail,
                empty_before,
                conv_values,
                conv_states,
                bias_steps,
                segment_whole,
            )
            return core(prepared, log_rates, skip_gains, segment_whole)

        if with_pull:
            gated, pull = jax.vjp(
                local_mixer, projected, smalls[0], smalls[1], smalls[2], smalls[3], smalls[4]
            )
        else:
            gated = local_mixer(projected, smalls[0], smalls[1], smalls[2], smalls[3], smalls[4])
            pull = None
        squares = unit_total(jnp.sum(gated * gated, axis=1))
        inverse = lax.rsqrt(squares / inner_total + epsilon)
        mixed = (gated * inverse[:, None] * gate_gain).astype(jnp.bfloat16)
        return (gathered, gated, inverse, mixed, pull)

    def run_backward(normed, segment_whole, grad_low, weights):
        gain, w_in, out_rows, smalls, gate_gain = weights
        gathered, gated, inverse, mixed, pull = mixed_rows(normed, segment_whole, weights, True)
        grad_rows = gather_rows(grad_low)
        grad_w_out = jnp.einsum("ti,td->id", mixed, grad_rows, preferred_element_type=jnp.float32)
        grad_mixed = jnp.einsum(
            "td,id->ti", grad_rows, out_rows, preferred_element_type=jnp.float32
        )
        grad_gate_gain = jnp.sum(grad_mixed * gated * inverse[:, None], axis=0)
        grad_unit = grad_mixed * gate_gain
        inner_products = unit_total(jnp.sum(grad_unit * gated, axis=1))
        grad_gated = (
            grad_unit * inverse[:, None]
            - gated * (inverse**3 * inner_products / inner_total)[:, None]
        )
        grad_projected, grad_conv_x, grad_conv_bc, grad_dt_bias, grad_a_log, grad_d_skip = pull(
            grad_gated
        )
        grad_low_proj = grad_projected.astype(jnp.bfloat16)
        grad_w_in = jnp.einsum(
            "td,tc->dc", gathered, grad_low_proj, preferred_element_type=jnp.float32
        )

        def input_term(start, number):
            return jnp.einsum("tc,dc->td", grad_low_proj, w_in, preferred_element_type=jnp.float32)

        grad_normed = row_total(input_term)
        return (
            grad_normed,
            (
                grad_w_in,
                grad_w_out,
                grad_conv_x,
                grad_conv_bc,
                grad_dt_bias,
                grad_a_log,
                grad_d_skip,
                grad_gate_gain,
            ),
        )

    empty_rows = jnp.zeros((local_rows, width), jnp.bfloat16)
    received = empty_rows
    kept_inputs = []
    kept_outputs = []
    kept_extra = []
    for step in range(micro + 1):
        weights = fetch()
        own_rows = x_input[step] if step < micro else empty_rows
        hidden = jnp.where(section_first, own_rows, received).astype(jnp.float32)
        batch_index = jnp.clip(step - section_index, 0, micro - 1)
        segment_whole = lax.dynamic_index_in_dim(segments_all, batch_index, 0, keepdims=False)
        scale = lax.rsqrt(jnp.mean(hidden * hidden, axis=1, keepdims=True) + epsilon)
        normed = (hidden * scale * weights[0]).astype(jnp.bfloat16)
        run_out_rows = weights[2]
        run_mixed = mixed_rows(normed, segment_whole, weights, False)[3]

        def branch_term(start, number):
            return jnp.dot(run_mixed, run_out_rows, preferred_element_type=jnp.float32)

        branch = row_total(branch_term)
        extra = ()
        produced = hidden + branch
        kept_inputs.append(hidden)
        kept_outputs.append(produced)
        kept_extra.append(extra)
        if step < micro:
            received = passed_along(produced.astype(jnp.bfloat16), "section", 1)
    inputs_stack = jnp.stack(kept_inputs)
    outputs_stack = jnp.stack(kept_outputs)
    inputs_by_batch = jnp.where(section_first, inputs_stack[:micro], inputs_stack[1:])
    outputs_by_batch = jnp.where(section_first, outputs_stack[:micro], outputs_stack[1:])
    extras_by_batch = jax.tree.map(
        lambda stacked: jnp.where(section_first, stacked[:micro], stacked[1:]),
        stack_steps(kept_extra),
    )
    returned = empty_rows
    totals = None
    grads_list = []
    for step in range(micro + 1):
        weights = fetch()
        batch_raw = micro - step - section_index
        live = ((batch_raw >= 0) & (batch_raw < micro)).astype(jnp.float32)
        batch_index = jnp.clip(batch_raw, 0, micro - 1)
        hidden = lax.dynamic_index_in_dim(inputs_by_batch, batch_index, 0, keepdims=False)
        final_rows = lax.dynamic_index_in_dim(outputs_by_batch, batch_index, 0, keepdims=False)
        extra = jax.tree.map(
            lambda stacked: lax.dynamic_index_in_dim(stacked, batch_index, 0, keepdims=False),
            extras_by_batch,
        )
        target = lax.dynamic_index_in_dim(teacher, batch_index, 0, keepdims=False)
        segment_whole = lax.dynamic_index_in_dim(segments_all, batch_index, 0, keepdims=False)
        length = lax.dynamic_index_in_dim(lengths_all, batch_index, 0, keepdims=False)
        counted_rows = (positions < length).astype(jnp.float32)
        loss_grad = 2.0 * loss_weight * live * counted_rows[:, None] * (final_rows - target)
        grad_out = jnp.where(section_first, returned.astype(jnp.float32), loss_grad)
        gain = weights[0]
        scale = lax.rsqrt(jnp.mean(hidden * hidden, axis=1, keepdims=True) + epsilon)
        normed = (hidden * scale * gain).astype(jnp.bfloat16)
        grad_normed, layer_grads = run_backward(
            normed, segment_whole, grad_out.astype(jnp.bfloat16), weights
        )
        grad_gain = jnp.sum(grad_normed * hidden * scale, axis=0)
        weighted = grad_normed * gain
        grad_hidden = (
            grad_out
            + scale * weighted
            - hidden * scale**3 * jnp.mean(weighted * hidden, axis=1, keepdims=True)
        )
        step_grads = (grad_gain,) + layer_grads
        if totals is None:
            totals = step_grads
        else:
            totals = jax.tree.map(lambda left, right: left + right, totals, step_grads)
        grads_list.append(grad_hidden)
        if step < micro:
            returned = passed_along(grad_hidden.astype(jnp.bfloat16), "section", -1)
    back_stack = jnp.stack(grads_list)
    boundary = jnp.where(section_first, back_stack[1:][::-1], back_stack[:micro][::-1])
    (
        grad_gain,
        grad_w_in,
        grad_w_out,
        grad_conv_x,
        grad_conv_bc,
        grad_dt_bias,
        grad_a_log,
        grad_d_skip,
        grad_gate_gain,
    ) = totals
    inner_width = grad_conv_x.shape[1]
    grad_zx = jnp.stack(
        [grad_w_in[:, :inner_width], grad_w_in[:, inner_width : 2 * inner_width]], axis=1
    )
    state_end = 2 * inner_width + 2 * STATE
    grad_bc = grad_w_in[:, 2 * inner_width : state_end]
    grad_dt = grad_w_in[:, state_end:]
    shares = (
        lax.psum_scatter(grad_gain[None], "dp", scatter_dimension=1, tiled=True),
        lax.psum_scatter(grad_zx[None], "dp", scatter_dimension=1, tiled=True),
        lax.psum_scatter(grad_bc[None], "dp", scatter_dimension=1, tiled=True),
        lax.psum_scatter(grad_dt[None], "dp", scatter_dimension=1, tiled=True),
        lax.psum_scatter(grad_w_out[None], "dp", scatter_dimension=2, tiled=True),
    )
    small_sums = lax.psum(
        (grad_conv_x, grad_conv_bc, grad_dt_bias, grad_a_log, grad_d_skip, grad_gate_gain), "dp"
    )
    shared = lax.psum((shares[0], shares[2], small_sums[1]), "tensor")
    return (
        outputs_by_batch.astype(jnp.bfloat16)[None],
        boundary[None],
        shared[0],
        shares[1],
        shared[1],
        shares[3],
        small_sums[0][None],
        shared[2][None],
        small_sums[2][None],
        small_sums[3][None],
        small_sums[4][None],
        small_sums[5][None],
        shares[4],
    )


def solution(mesh):
    placed = (
        P(None, ("dp", "tensor"), None),
        P(None, ("dp", "tensor"), None),
        P(None, "dp", None),
        P(),
        P("section", "dp"),
        P("section", "dp", None, "tensor"),
        P("section", "dp", None),
        P("section", "dp", "tensor"),
        P("section", None, "tensor"),
        P("section", None, None),
        P("section", None),
        P("section", None),
        P("section", None),
        P("section", "tensor"),
        P("section", "tensor", "dp"),
    )
    return jax.shard_map(
        body,
        mesh=mesh,
        in_specs=placed,
        out_specs=(
            P("section", None, ("dp", "tensor"), None),
            P("section", None, ("dp", "tensor"), None),
            P("section", "dp"),
            P("section", "dp", None, "tensor"),
            P("section", "dp", None),
            P("section", "dp", "tensor"),
            P("section", None, "tensor"),
            P("section", None, None),
            P("section", "tensor"),
            P("section", "tensor"),
            P("section", "tensor"),
            P("section", "tensor"),
            P("section", "tensor", "dp"),
        ),
        check_vma=False,
    )
```

profile of v0, /device:TPU:0, one launch (start us, length us, event | category | flops | bytes accessed | tf_op | source)
XLA Modules:
  0.0 2459.8 jit_solution(274596667096085776)
XLA Ops:
  12.0 23.2 all-reduce.117
  39.8 32.3 %all_gather.31 = bf16[1,768,256]{2,1,0:T(8,128)(2,1)S(1)} all-gather(bf16[1,96,256]{2,1,0:T(8,128)(2,1)S(1)} %copy-done.256), channel_id=1, replica_groups=mesh['section'=2,'dp'=8,'tensor'=2] {'dp'}, dimensions={1}, use_global_device_ids=true | all-gather | bytes 442368 | tf_op jit(solution)/shard_map/all_gather | solution.py:153
  72.2 30.6 %all_gather.32 = bf16[1,768,12]{2,1,0:T(8,128)(2,1)S(1)} all-gather(bf16[1,96,12]{2,1,0:T(8,128)(2,1)S(1)} %copy.746), channel_id=1, replica_groups=mesh['section'=2,'dp'=8,'tensor'=2] {'dp'}, dimensions={1}, use_global_device_ids=true | all-gather | bytes 20736 | tf_op jit(solution)/shard_map/all_gather | solution.py:154
  174.0 44.0 %while.201 = (s32[]{:T(128)}, f32[12,64,128]{2,1,0:T(8,128)S(1)}, s32[]{:T(128)}, f32[4,256,12,64]{1,3,2,0:T(8,128)}, f32[4,256,12]{2,1,0:T(8,128)}, /*index=5*/...) while((s32[]{:T(128)}, f32[12,64,128]{2,1,0:T(8,128)S(1)}, ...), condition=%wide.region_4.5_spmd.clone, body=%wide.region_3.4_spmd.clone.sunk | while | flops 302583328 | bytes 2560338 | solution.py:72
  220.2 16.7 bitcast_add_fusion.14
  256.6 23.5 reduce-scatter.13.cloned.1.call-done
  292.6 25.3 %all-gather.18.cloned.1.call-done = bf16[1024,768]{1,0:T(8,128)(2,1)} async-done(((bf16[512,768]{1,0:T(8,128)(2,1)}), bf16[1024,768]{1,0:T(8,128)(2,1)}) %all-gather.18.cloned.1.call-update) | async-done | bytes 1572880 | tf_op jit(solution)/shard_map/all_gather | solution.py:180
  380.2 43.6 %while.202 = (s32[]{:T(128)}, f32[12,64,128]{2,1,0:T(8,128)S(1)}, s32[]{:T(128)}, f32[4,256,12,64]{1,3,2,0:T(8,128)}, f32[4,256,12]{2,1,0:T(8,128)}, /*index=5*/...) while((s32[]{:T(128)}, f32[12,64,128]{2,1,0:T(8,128)S(1)}, ...), condition=%wide.region_12.13_spmd.clone, body=%wide.region_11.12_spmd.clone.sunk | while | flops 302583328 | bytes 2560338 | solution.py:72
  423.8 17.2 bitcast_add_fusion.13
  460.5 26.2 %reduce-scatter.15.cloned.1.call-done = bf16[512,768]{1,0:T(8,128)(2,1)} async-done(((bf16[1024,768]{1,0:T(8,128)(2,1)}), bf16[512,768]{1,0:T(8,128)(2,1)}) %reduce-scatter.15.cloned.1.call-update) | async-done | bytes 786448 | tf_op jit(solution)/shard_map/reduce_scatter | solution.py:186
  498.9 24.8 %all-gather.20.cloned.1.call-done = bf16[1024,768]{1,0:T(8,128)(2,1)} async-done(((bf16[512,768]{1,0:T(8,128)(2,1)}), bf16[1024,768]{1,0:T(8,128)(2,1)}) %all-gather.20.cloned.1.call-update) | async-done | bytes 1572880 | tf_op jit(solution)/shard_map/all_gather | solution.py:180
  531.3 21.7 all-gather.22.cloned.1.call-done
  581.1 16.9 fusion.267
  618.9 38.2 %while.203 = (s32[]{:T(128)}, f32[12,64,128]{2,1,0:T(8,128)S(1)}, s32[]{:T(128)}, f32[4,256,12,64]{1,3,2,0:T(8,128)}, f32[4,256,12]{2,1,0:T(8,128)}, /*index=5*/...) while((s32[]{:T(128)}, f32[12,64,128]{2,1,0:T(8,128)S(1)}, ...), condition=%wide.region_20.21_spmd.clone, body=%wide.region_19.20_spmd.clone.sunk | while | flops 302583328 | bytes 2560338 | solution.py:72
  657.1 17.2 bitcast_add_fusion.12
  711.9 85.7 %while.204 = (s32[]{:T(128)}, f32[12,64,128]{2,1,0:T(8,128)}, s32[]{:T(128)}, f32[4,256,12,64]{1,3,2,0:T(8,128)}, f32[4,256,12]{1,2,0:T(8,128)}, /*index=5*/f32[...) while((s32[]{:T(128)}, f32[12,64,128]{2,1,0:T(8,128)}, ...), condition=%wide.region_29.31_spmd.clone, body=%wide.region_28.30_spmd.clone.sunk | while | flops 302684704 | bytes 5127235 | solution.py:72
  797.6 17.2 bitcast_add_fusion.11
  840.6 23.5 reduce-scatter.17.cloned.1.call-done
  870.6 27.3 %all-gather.24.cloned.1.call-done = bf16[1024,768]{1,0:T(8,128)(2,1)} async-done(((bf16[512,768]{1,0:T(8,128)(2,1)}), bf16[1024,768]{1,0:T(8,128)(2,1)}) %all-gather.24.cloned.1.call-update) | async-done | bytes 1572880 | tf_op jit(solution)/shard_map/all_gather | solution.py:180
  927.3 20.4 fusion.154
  950.5 77.9 %while.205 = (s32[]{:T(128)}, f32[12,64,128]{2,1,0:T(8,128)}, f32[4,256,12]{1,2,0:T(8,128)}, f32[4,256,128]{2,1,0:T(8,128)}, f32[4,12,64,128]{3,2,1,0:T(8,128)},...) while((s32[]{:T(128)}, f32[12,64,128]{2,1,0:T(8,128)}, ...), condition=%wide.region_37.39_spmd.clone, body=%wide.region_34.38_spmd.clone.sunk | while | flops 605460480 | bytes 7069216 | solution.py:72
  1039.0 12.8 multiply_reduce_fusion.32
  1052.5 10.1 reduce-window.74
  1104.9 26.2 %reduce-scatter.19.cloned.1.call-done = bf16[512,768]{1,0:T(8,128)(2,1)} async-done(((bf16[1024,768]{1,0:T(8,128)(2,1)}), bf16[512,768]{1,0:T(8,128)(2,1)}) %reduce-scatter.19.cloned.1.call-update) | async-done | bytes 786448 | tf_op jit(solution)/shard_map/reduce_scatter | solution.py:186
  1146.4 19.2 all-gather.26.cloned.1.call-done
  1192.9 10.3 fusion.265
  1228.3 88.9 %while.206 = (s32[]{:T(128)}, f32[12,64,128]{2,1,0:T(8,128)}, s32[]{:T(128)}, f32[4,256,12,64]{1,3,2,0:T(8,128)}, f32[4,256,12]{1,2,0:T(8,128)}, /*index=5*/f32[...) while((s32[]{:T(128)}, f32[12,64,128]{2,1,0:T(8,128)}, ...), condition=%wide.region_52.54_spmd.clone, body=%wide.region_51.53_spmd.clone.sunk | while | flops 302684704 | bytes 5126219 | solution.py:72
  1317.2 17.2 bitcast_add_fusion.9
  1360.1 9.5 multiply_reduce_fusion.10
  1379.1 20.4 fusion.156
  1402.3 80.5 %while.207 = (s32[]{:T(128)}, f32[12,64,128]{2,1,0:T(8,128)}, f32[4,256,12]{1,2,0:T(8,128)}, f32[4,256,128]{2,1,0:T(8,128)}, f32[4,12,64,128]{3,2,1,0:T(8,128)},...) while((s32[]{:T(128)}, f32[12,64,128]{2,1,0:T(8,128)}, ...), condition=%wide.region_60.62_spmd.clone, body=%wide.region_57.61_spmd.clone.sunk | while | flops 605460480 | bytes 7101568 | solution.py:72
  1493.5 13.4 multiply_reduce_fusion.28
  1508.3 10.1 reduce-window.80
  1567.1 9.1 fusion.585
  1576.2 16.3 reduce-scatter.21.cloned.1.call-done
  1615.9 10.7 all-gather.30.cloned.1.call-done
  1645.1 9.9 fusion.263
  1681.2 91.4 %while.208 = (s32[]{:T(128)}, f32[12,64,128]{2,1,0:T(8,128)}, s32[]{:T(128)}, f32[4,256,12,64]{1,3,2,0:T(8,128)}, f32[4,256,12]{1,2,0:T(8,128)}, /*index=5*/f32[...) while((s32[]{:T(128)}, f32[12,64,128]{2,1,0:T(8,128)}, ...), condition=%wide.region_75.77_spmd.clone, body=%wide.region_74.76_spmd.clone.sunk | while | flops 302684704 | bytes 5127235 | solution.py:72
  1772.5 17.2 bitcast_add_fusion.7
  1833.5 20.4 fusion.158
  1856.6 78.6 %while.209 = (s32[]{:T(128)}, f32[12,64,128]{2,1,0:T(8,128)}, f32[4,256,12]{1,2,0:T(8,128)}, f32[4,256,128]{2,1,0:T(8,128)}, f32[4,12,64,128]{3,2,1,0:T(8,128)},...) while((s32[]{:T(128)}, f32[12,64,128]{2,1,0:T(8,128)}, ...), condition=%wide.region_83.85_spmd.clone, body=%wide.region_80.84_spmd.clone.sunk | while | flops 605460480 | bytes 7069216 | solution.py:72
  1945.9 12.8 multiply_reduce_fusion.24
  1959.3 10.2 reduce-window.86
  2016.9 11.1 add_add_fusion
  2079.3 37.7 %all-reduce.121 = (f32[1,5,768]{2,0,1:T(1,128)}, f32[5,256]{1,0:T(8,128)S(1)}, f32[1,12]{1,0:T(1,128)}, f32[1,12]{1,0:T(1,128)}, f32[1,12]{1,0:T(1,128)}, /*index=5*/f32[1,768]{1,0:T(1,128)}) all-reduce(f32[1,5,768]{2,0,1:T(1,128)S(1)} %broadcast_in_dim.478, ...), channel_id=1, replica_groups=mesh['section'=2,'dp'=8,'tensor'=2] {'dp'}, use_global_device_ids=true, to_apply=%region_118.120 | all-reduce | flops 5924 | bytes 47392 | tf_op jit(solution)/shard_map/psum | solution.py:366
  2124.4 43.2 %reduce-scatter.25.cloned.1.call-done = f32[96,1]{1,0:T(8,128)} async-done(((f32[768,1]{1,0:T(8,128)}), f32[96,1]{1,0:T(8,128)}) %reduce-scatter.25.cloned.1.call-update) | async-done | bytes 400
  2174.1 253.6 %all-reduce.130.cloned.1.call-done = (f32[1,768,2,768]{3,2,0,1:T(2,128)}, f32[1,768,256]{2,0,1:T(1,128)}, f32[1,768,768]{1,0,2:T(1,128)}) async-done(((f32[1,768,2,768]{3,2,0,1:T(2,128)}, f32[1,768,256]{2,0,1:T(1,128)}, f32[1,768,768]{1,0,2:T(1,128)}), (f32[1,768,2,768]{3,2,0,1:T(2,128)}, f32[1,768,256]{2,0,1:T(1,128)}, f32[1,768,768]{1,0,2:T(1,128)})) %all-reduce.130.cloned.1.call-update) | async-done | bytes 7864336
  2432.9 18.3 all-reduce.128.cloned.1.call-done
  (1781 shorter events, 1422.9 us)
Async XLA Ops:
  7.2 100.3 %copy-start = (f32[1,24]{1,0:T(1,128)S(1)}, f32[1,24]{1,0:T(1,128)}, u32[]{:S(2)}) copy-start(f32[1,24]{1,0:T(1,128)} %param.44) | copy-start | bytes 292
  7.2 32.6 %copy-start.256 = (bf16[1,96,256]{2,1,0:T(8,128)(2,1)S(1)}, bf16[1,96,256]{2,1,0:T(8,128)(2,1)}, u32[]{:S(2)}) copy-start(bf16[1,96,256]{2,1,0:T(8,128)(2,1)} %param.40) | copy-start | bytes 147460
  7.2 64.9 %copy-start.321 = (bf16[1,96,12]{1,2,0:T(8,128)(2,1)S(1)}, bf16[1,96,12]{1,2,0:T(8,128)(2,1)}, u32[]{:S(2)}) copy-start(bf16[1,96,12]{1,2,0:T(8,128)(2,1)} %param.41) | copy-start | bytes 6916
  7.2 96.1 %copy-start.286 = (s32[2,1,1024]{2,1,0:T(1,128)S(1)}, s32[2,1,1024]{2,1,0:T(1,128)}, u32[]{:S(2)}) copy-start(s32[2,1,1024]{2,1,0:T(1,128)} %param.36) | copy-start | bytes 24580
  7.2 98.9 %copy-start.315 = (bf16[1,5,768]{2,1,0:T(8,128)(2,1)S(1)}, bf16[1,5,768]{2,1,0:T(8,128)(2,1)}, u32[]{:S(2)}) copy-start(bf16[1,5,768]{2,1,0:T(8,128)(2,1)} %param.42) | copy-start | bytes 23044
  7.2 99.6 %copy-start.319 = (bf16[1,5,256]{2,1,0:T(8,128)(2,1)S(1)}, bf16[1,5,256]{2,1,0:T(8,128)(2,1)}, u32[]{:S(2)}) copy-start(bf16[1,5,256]{2,1,0:T(8,128)(2,1)} %param.43) | copy-start | bytes 7684
  7.2 100.8 %copy-start.343 = (f32[1,24]{1,0:T(1,128)S(1)}, f32[1,24]{1,0:T(1,128)}, u32[]{:S(2)}) copy-start(f32[1,24]{1,0:T(1,128)} %param.45) | copy-start | bytes 292
  7.3 100.8 %copy-start.344 = (f32[1,24]{1,0:T(1,128)S(1)}, f32[1,24]{1,0:T(1,128)}, u32[]{:S(2)}) copy-start(f32[1,24]{1,0:T(1,128)} %param.46) | copy-start | bytes 292
  7.3 101.6 %copy-start.340 = (bf16[1,768]{1,0:T(2,128)(2,1)S(1)}, bf16[1,768]{1,0:T(2,128)(2,1)}, u32[]{:S(2)}) copy-start(bf16[1,768]{1,0:T(2,128)(2,1)} %param.47) | copy-start | bytes 4612
  7.3 103.7 %all-gather.14.cloned.1.call-start = ((), (), s32[]{:S(2)}) async-start(), calls=%async_computation.9 | async-start | bytes 2654208 | tf_op jit(solution)/shard_map/all_gather | solution.py:152
  9.1 103.7 %all-gather.12.cloned.1.call-start = ((), (), s32[]{:S(2)}) async-start(), calls=%async_computation.8 | async-start | bytes 2359296 | tf_op jit(solution)/shard_map/all_gather | solution.py:180
  38.9 212.3 %all-gather.16.cloned.1.call-start = ((), (), s32[]{:S(2)}) async-start(), calls=%async_computation.10 | async-start | bytes 1327104 | tf_op jit(solution)/shard_map/all_gather | solution.py:155
  39.7 240.4 %reduce-scatter.13.cloned.1.call-start = ((), (), s32[]{:S(2)}) async-start(), calls=%async_computation.11 | async-start | bytes 2359296 | tf_op jit(solution)/shard_map/reduce_scatter | solution.py:186
  72.1 40.7 %copy-start.173 = (bf16[1,768,256]{2,1,0:T(8,128)(2,1)}, bf16[1,768,256]{2,1,0:T(8,128)(2,1)S(1)}, u32[]{:S(2)}) copy-start(bf16[1,768,256]{2,1,0:T(8,128)(2,1)S(1)} %all_gather.31) | copy-start | bytes 1179652
  106.8 474.3 %copy-start.130 = (f32[768]{0:T(1024)}, f32[768]{0:T(1024)S(1)}, u32[]{:S(2)}) copy-start(f32[768]{0:T(1024)S(1)} %get-tuple-element.2433) | copy-start | bytes 9220
  106.8 474.3 %copy-start.134 = (f32[768]{0:T(1024)}, f32[768]{0:T(1024)S(1)}, u32[]{:S(2)}) copy-start(f32[768]{0:T(1024)S(1)} %get-tuple-element.2434) | copy-start | bytes 9220
  256.4 61.5 %all-gather.18.cloned.1.call-start = ((), (), s32[]{:S(2)}) async-start(), calls=%async_computation.12 | async-start | bytes 2359296 | tf_op jit(solution)/shard_map/all_gather | solution.py:180
  282.7 3.8 collective-permute-start
  290.5 196.2 %reduce-scatter.15.cloned.1.call-start = ((), (), s32[]{:S(2)}) async-start(), calls=%async_computation.13 | async-start | bytes 2359296 | tf_op jit(solution)/shard_map/reduce_scatter | solution.py:186
  460.4 63.2 %all-gather.20.cloned.1.call-start = ((), (), s32[]{:S(2)}) async-start(), calls=%async_computation.14 | async-start | bytes 2359296 | tf_op jit(solution)/shard_map/all_gather | solution.py:180
  489.2 3.8 collective-permute-start.1
  496.3 56.8 %all-gather.22.cloned.1.call-start = ((), (), s32[]{:S(2)}) async-start(), calls=%async_computation.16 | async-start | bytes 2359296 | tf_op jit(solution)/shard_map/all_gather | solution.py:180
  497.0 367.1 %reduce-scatter.17.cloned.1.call-start = ((), (), s32[]{:S(2)}) async-start(), calls=%async_computation.15 | async-start | bytes 2359296 | tf_op jit(solution)/shard_map/reduce_scatter | solution.py:186
  598.1 311.6 %copy-start.9 = (f32[1024,768]{0,1:T(8,128)}, f32[1024,768]{0,1:T(8,128)S(1)}, u32[]{:S(2)}) copy-start(f32[1024,768]{0,1:T(8,128)S(1)} %get-tuple-element.2739) | copy-start | bytes 9437188
  837.9 60.0 %all-gather.24.cloned.1.call-start = ((), (), s32[]{:S(2)}) async-start(), calls=%async_computation.17 | async-start | bytes 2359296 | tf_op jit(solution)/shard_map/all_gather | solution.py:180
  870.5 260.5 %reduce-scatter.19.cloned.1.call-start = ((), (), s32[]{:S(2)}) async-start(), calls=%async_computation.18 | async-start | bytes 2359296 | tf_op jit(solution)/shard_map/reduce_scatter | solution.py:186
  870.6 39.0 %copy-start.311 = (f32[1024]{0:T(1024)}, f32[1024]{0:T(1024)S(1)}, u32[]{:S(2)}) copy-start(f32[1024]{0:T(1024)S(1)} %add_rsqrt_fusion.2) | copy-start | bytes 12292
  1098.4 32.7 %copy-start.3 = (f32[2,512,768]{2,1,0:T(8,128)S(1)}, f32[2,512,768]{2,1,0:T(8,128)}, u32[]{:S(2)}) copy-start(f32[2,512,768]{2,1,0:T(8,128)} %copy-done.2) | copy-start | bytes 9437188
  1098.4 32.6 %copy-start.152 = (f32[768]{0:T(1024)S(1)}, f32[768]{0:T(1024)}, u32[]{:S(2)}) copy-start(f32[768]{0:T(1024)} %copy-done.149) | copy-start | bytes 9220
  1098.5 32.6 %copy-start.269 = (f32[512]{0:T(512)S(1)}, f32[512]{0:T(512)}, u32[]{:S(2)}) copy-start(f32[512]{0:T(512)} %copy-done.268) | copy-start | bytes 6148
  1104.9 60.8 %all-gather.26.cloned.1.call-start = ((), (), s32[]{:S(2)}) async-start(), calls=%async_computation.19 | async-start | bytes 2359296 | tf_op jit(solution)/shard_map/all_gather | solution.py:180
  1138.3 210.1 %all-gather.28.cloned.1.call-start = ((), (), s32[]{:S(2)}) async-start(), calls=%async_computation.20 | async-start | bytes 2359296 | tf_op jit(solution)/shard_map/all_gather | solution.py:180
  1138.3 4.5 collective-permute-start.2
  1146.4 446.2 %reduce-scatter.21.cloned.1.call-start = ((), (), s32[]{:S(2)}) async-start(), calls=%async_computation.21 | async-start | bytes 2359296 | tf_op jit(solution)/shard_map/reduce_scatter | solution.py:186
  1176.4 37.1 %copy-start.123 = (f32[4,256,12]{1,2,0:T(8,128)}, f32[4,256,12]{1,2,0:T(8,128)S(1)}, u32[]{:S(2)}) copy-start(f32[4,256,12]{1,2,0:T(8,128)S(1)} %get-tuple-element.2826) | copy-start | bytes 147460
  1566.3 60.3 %all-gather.30.cloned.1.call-start = ((), (), s32[]{:S(2)}) async-start(), calls=%async_computation.22 | async-start | bytes 2359296 | tf_op jit(solution)/shard_map/all_gather | solution.py:180
  1567.1 46.6 %copy-start.282 = (f32[512]{0:T(512)}, f32[512]{0:T(512)S(1)}, u32[]{:S(2)}) copy-start(f32[512]{0:T(512)S(1)} %fusion.561) | copy-start | bytes 6148
  1599.3 204.3 %all-gather.32.cloned.1.call-start = ((), (), s32[]{:S(2)}) async-start(), calls=%async_computation.23 | async-start | bytes 2359296 | tf_op jit(solution)/shard_map/all_gather | solution.py:180
  1604.8 8.9 collective-permute-start.3
  1615.8 429.5 %reduce-scatter.23.cloned.1.call-start = ((), (), s32[]{:S(2)}) async-start(), calls=%async_computation.24 | async-start | bytes 2359296 | tf_op jit(solution)/shard_map/reduce_scatter | solution.py:186
  1655.0 160.3 %copy-start.11 = (f32[1024,768]{0,1:T(8,128)}, f32[1024,768]{0,1:T(8,128)S(1)}, u32[]{:S(2)}) copy-start(f32[1024,768]{0,1:T(8,128)S(1)} %get-tuple-element.2725) | copy-start | bytes 9437188
  2012.5 104.5 %reduce-scatter.27.cloned.1.call-start = ((), (), s32[]{:S(2)}) async-start(), calls=%async_computation.27 | async-start | bytes 442368
  2038.5 129.1 %reduce-scatter.25.cloned.1.call-start = ((), (), s32[]{:S(2)}) async-start(), calls=%async_computation.26 | async-start | bytes 442368
  2048.1 379.6 %all-reduce.130.cloned.1.call-start = ((), (), s32[]{:S(2)}) async-start(), calls=%async_computation.28 | async-start | bytes 15728640
  2071.2 380.0 %all-reduce.128.cloned.1.call-start = ((), (), s32[]{:S(2)}) async-start(), calls=%async_computation.25 | async-start | bytes 196608 | tf_op jit(solution)/shard_map/psum | solution.py:369
  2073.9 44.5 %copy-start.283 = (f32[512]{0:T(512)S(1)}, f32[512]{0:T(512)}, u32[]{:S(2)}) copy-start(f32[512]{0:T(512)} %copy-done.282) | copy-start | bytes 6148
  2074.0 44.5 %copy-start.316 = (f32[512]{0:T(512)S(1)}, f32[512]{0:T(512)}, u32[]{:S(2)}) copy-start(f32[512]{0:T(512)} %get-tuple-element.2870) | copy-start | bytes 6148
  2122.3 330.4 %copy-start.1 = (f32[1,24]{1,0:T(1,128)S(1)}, f32[1,24]{1,0:T(1,128)}, u32[]{:S(2)}) copy-start(f32[1,24]{1,0:T(1,128)} %param.44) | copy-start | bytes 292
  (353 other events, 2774.4 us)
Sparse Core Ops, SparseCore 0:
  10.9 60.5 all-gather.13
  73.6 25.7 all-gather.11
  101.5 41.0 all-gather.15
  256.5 23.5 reduce-scatter.12
  290.6 27.2 all-gather.17
  460.6 26.0 reduce-scatter.14
  496.4 27.2 all-gather.19
  525.8 27.2 all-gather.21
  838.1 26.0 reduce-scatter.16
  870.7 27.2 all-gather.23
  1105.0 26.0 reduce-scatter.18
  1138.4 27.2 all-gather.25
  1167.2 27.2 all-gather.27
  1566.4 26.0 reduce-scatter.20
  1599.4 27.2 all-gather.29
  1628.1 27.2 all-gather.31
  2012.6 26.0 reduce-scatter.22
  2041.9 61.3 reduce-scatter.26
  2107.1 60.4 reduce-scatter.24
  2171.8 255.8 all-reduce.129
  2431.1 20.0 all-reduce.127
where the time goes:
time: 2490 us; the launch traced here: 2460 us
  local copies, waits for them, and re-layouts  574 us (23%)
  matrix products  572 us (23%)
  waiting for transfers between devices  568 us (23%)
  other arithmetic  516 us (21%)
  blocking collectives  169 us (7%)
  loops' own time  32.1 us (1%)
    unnamed x24, waiting for transfers between devices  299 us
    dot_general x12, matrix products, block_scan(): jnp.einsum('chij,cjhp->cihp', factors * scores[:, None], scaled, precisio...  203 us
    dot_general x48, matrix products, carry_step(): jnp.einsum('is,hps->ihp', c_block, state, precision=lax.Precision.HIGHEST)  134 us
    all_gather x9, waiting for transfers between devices, gather_rows(): return lax.all_gather(rows_here, 'tensor', axis=0, tiled=True)  129 us
    reduce_scatter x6, waiting for transfers between devices, row_total(): lax.psum_scatter(term(jnp.int32(0), local_rows * lax.axis_size('tensor'))...  116 us
    dynamic_update_slice x72, local copies, waits for them, and re-layouts, block_scan(): lax.scan(carry_step, (start_state, start_segment), (log_decay, c_rows, se...  99.1 us
    unnamed x721, local copies, waits for them, and re-layouts  77.7 us
    dot_general x12, matrix products, block_scan(): jnp.einsum('cjhp,cjs->chps', tail[..., None] * scaled, b_rows, precision=...  69.1 us
  transfers between devices with their start and end apart: 25, of which 17 were waited for; matrix products, arithmetic and copies ran while one was open for 24% of the time, Pallas kernels for 0%

commit v1 on v0

v1 whole, which is shorter than its diff:
```python
import functools

import jax
import jax.numpy as jnp
import numpy as np
from jax import lax
from jax.experimental import pallas as pl
from jax.experimental.pallas import tpu as pltpu
from jax.sharding import PartitionSpec as P

HEAD_DIM = 64
STATE = 128
SPAN = 256
LANES = 128

epsilon = 1e-05
f32 = jnp.float32
bf16 = jnp.bfloat16


def nn(left, right):
    return lax.dot_general(left, right, (((1,), (0,)), ((), ())), preferred_element_type=f32)


def nt(left, right):
    return lax.dot_general(left, right, (((1,), (1,)), ((), ())), preferred_element_type=f32)


def tn(left, right):
    return lax.dot_general(left, right, (((0,), (0,)), ((), ())), preferred_element_type=f32)


def high_low(value):
    high = value.astype(bf16)
    return high, (value - high.astype(f32)).astype(bf16)


def spread(per_head, spreader):
    return nn(jnp.concatenate(high_low(per_head), axis=1), spreader)


def gathered_heads(units, spreader):
    high, low = high_low(units)
    once = spreader[:LANES]
    return nt(high, once) + nt(low, once)


def running_sum(triangle, value):
    high = value.astype(bf16)
    rest = value - high.astype(f32)
    middle = rest.astype(bf16)
    low = (rest - middle.astype(f32)).astype(bf16)
    sums = nn(triangle, jnp.concatenate([high, middle, low], axis=1))
    return sums[:, :LANES] + sums[:, LANES : 2 * LANES] + sums[:, 2 * LANES :]


def softplus(value):
    return jnp.maximum(value, 0.0) + jnp.log1p(jnp.exp(-jnp.abs(value)))


def moved_down(block, edge, lag):
    return jnp.concatenate([edge, block], axis=0)[8 - lag : 8 - lag + block.shape[0]]


def moved_up(block, edge, lag):
    return jnp.concatenate([block, edge], axis=0)[lag : lag + block.shape[0]]


def decay_parts(steps_in, head_rows, marks, heads):
    lane = lax.broadcasted_iota(jnp.int32, (1, LANES), 1)
    live = lane < heads
    shifted = steps_in + head_rows[0:1, :LANES]
    steps = jnp.where(live, softplus(shifted), 0.0)
    rates = head_rows[1:2, :LANES]
    log_steps = -steps * rates
    row = lax.broadcasted_iota(jnp.int32, (SPAN, SPAN), 0)
    column = lax.broadcasted_iota(jnp.int32, (SPAN, SPAN), 1)
    lower = (row >= column).astype(bf16)
    logs = running_sum(lower, log_steps)
    last = logs[SPAN - 1 : SPAN]
    entry = jnp.exp(logs) * marks[:, 3:4]
    tail = jnp.exp(last - logs) * marks[:, 4:5]
    through = jnp.exp(last) * marks[SPAN - 1 : SPAN, 3:4]
    entry = jnp.where(live, entry, 0.0)
    tail = jnp.where(live, tail, 0.0)
    through = jnp.where(live, through, 0.0)
    return shifted, steps, log_steps, logs, entry, tail, through, row, column


def linked_mask(row, column, marks, segment_row):
    linked = (row >= column) & (marks[:, 5:6] == segment_row)
    return jnp.where(linked, 0.0, -1e30)


def gain_row(weights):
    return jnp.transpose(weights[:, 384:512].astype(f32))[64:65, :]


def forward_kernel(second, heads, *refs):
    if second:
        (h_ref, own_ref, other_ref), refs = refs[:3], refs[3:]
    else:
        (h_ref,), refs = refs[:1], refs[1:]
    (a0, a1, b0, b1, o0, o1, marks_ref, segment_ref, small_ref, states_small_ref, head_ref, spread_ref), refs = refs[:12], refs[12:]
    if second:
        h_out, refs = refs[0], refs[1:]
    gate_ref, raw_ref, conv_ref, y_ref, raw_states_ref, conv_states_ref, steps_ref, entry_state_ref, part_ref = refs[:9]
    state, raw_edge, states_edge, gain = refs[9:]
    chunk = pl.program_id(0)
    half = gate_ref.shape[1] // 2

    @pl.when(chunk == 0)
    def _():
        state[...] = jnp.zeros_like(state)
        raw_edge[...] = jnp.zeros_like(raw_edge)
        states_edge[...] = jnp.zeros_like(states_edge)
        gain[0:1, :] = gain_row(b0[...])

    hidden = h_ref[...].astype(f32)
    if second:
        hidden = hidden + branch_of(own_ref, other_ref, 2 * half)[0]
        rounded = hidden.astype(bf16)
        h_out[...] = rounded
        hidden = rounded.astype(f32)
    scale = lax.rsqrt(jnp.mean(hidden * hidden, axis=1, keepdims=True) + epsilon)
    normed = (hidden * scale * gain[0:1, :]).astype(bf16)
    first_a = nn(normed, a0[...])
    second_a = nn(normed, a1[...])
    first_b = nn(normed, b0[...])
    second_b = nn(normed, b1[...])
    gate = jnp.concatenate([first_a[:, :half], second_a[:, :half]], axis=1)
    raw = jnp.concatenate([first_b[:, :half], second_b[:, :half]], axis=1)
    marks = marks_ref[...]
    turned = marks[0:1, 10:11] > 0.5
    first_states, second_states = first_a[:, half:], second_a[:, half:]
    raw_states = jnp.concatenate(
        [jnp.where(turned, second_states, first_states), jnp.where(turned, first_states, second_states)], axis=1
    )
    lane = lax.broadcasted_iota(jnp.int32, (1, LANES), 1)
    steps_in = jnp.where(lane < heads // 2, first_b[:, half:], pltpu.roll(second_b[:, half:], heads // 2, 1))
    gate_ref[...] = gate
    raw_ref[...] = raw
    raw_states_ref[...] = raw_states
    steps_ref[...] = steps_in

    def conv(block, edge, taps):
        total = taps[4:5] + taps[3:4] * block
        for lag in (1, 2, 3):
            total = total + taps[3 - lag : 4 - lag] * (moved_down(block, edge, lag) * marks[:, lag - 1 : lag])
        return total

    taps = small_ref[...]
    conved = conv(raw, raw_edge[...], taps)
    conv_ref[...] = conved
    conved_states = conv(raw_states, states_edge[...], states_small_ref[...])
    conv_states_ref[...] = conved_states
    raw_edge[...] = raw[SPAN - 8 :]
    states_edge[...] = raw_states[SPAN - 8 :]
    values = conved * jax.nn.sigmoid(conved)
    states_in = conved_states * jax.nn.sigmoid(conved_states)
    b_rows = states_in[:, :STATE].astype(bf16)
    c_rows = states_in[:, STATE:].astype(bf16)
    _, steps, _, logs, entry, tail, through, row, column = decay_parts(steps_in, head_ref[...], marks, heads)
    spreader = spread_ref[...]
    spread_steps = spread(steps, spreader)
    scaled = values * spread_steps
    mask = linked_mask(row, column, marks, segment_ref[...])
    scores = nt(c_rows, b_rows)
    logs_across = jnp.transpose(logs)
    pieces = []
    for pair in range(heads // 2):
        mixes = []
        for head in (2 * pair, 2 * pair + 1):
            factor = jnp.exp(logs[:, head : head + 1] - logs_across[head : head + 1, :] + mask)
            mixes.append((factor * scores).astype(bf16))
        block = scaled[:, pair * LANES : (pair + 1) * LANES]
        left = jnp.where(lane < HEAD_DIM, block, 0.0).astype(bf16)
        right = jnp.where(lane < HEAD_DIM, 0.0, block).astype(bf16)
        pieces.append(nn(jnp.concatenate(mixes, axis=1), jnp.concatenate([left, right], axis=0)))
    inside = jnp.concatenate(pieces, axis=1)
    held = state[...]
    entry_state_ref[0] = held
    across = nn(c_rows, held.astype(bf16)) * spread(entry, spreader)
    through_row = spread(jnp.broadcast_to(through, (8, LANES)), spreader)[0:1]
    state[...] = through_row * held + tn(b_rows, (spread(tail, spreader) * scaled).astype(bf16))
    y = inside + across + taps[6:7] * values
    y_ref[...] = y
    gated = y * (gate * jax.nn.sigmoid(gate))
    squares = jnp.sum(gated * gated, axis=1, keepdims=True)
    weighted = (gated * taps[5:6]).astype(bf16)
    part = nt(weighted[:, :half], o0[...]) + nt(weighted[:, half:], o1[...])
    width = part.shape[1]
    part_ref[:, :width] = part.astype(bf16)
    high, low = high_low(squares)
    part_ref[:, width:] = jnp.where(lane == 0, high, jnp.where(lane == 1, low, jnp.zeros_like(low)))


def branch_of(own_ref, other_ref, units):
    width = own_ref.shape[1] - LANES
    own = own_ref[...].astype(f32)
    other = other_ref[...].astype(f32)
    total = own[:, :width] + other[:, :width]
    own_squares = own[:, width : width + 1] + own[:, width + 1 : width + 2]
    other_squares = other[:, width : width + 1] + other[:, width + 1 : width + 2]
    inverse = lax.rsqrt((own_squares + other_squares) / (2 * units) + epsilon)
    return total * inverse, total, inverse


def backward_kernel(second, heads, *refs):
    if second:
        (h_ref, own_ref, other_ref, target_ref), refs = refs[:4], refs[4:]
    else:
        (h_ref, own_ref, other_ref, next_h_ref, next_out_ref, grad_own_ref, grad_other_ref, next_gain_ref), refs = refs[:8], refs[8:]
    (a0, a1, b0, b1, o0, o1, marks_ref, segment_ref, small_ref, states_small_ref, head_ref, spread_ref), refs = refs[:12], refs[12:]
    (gate_ref, raw_ref, conv_ref, y_ref, raw_states_ref, conv_states_ref, steps_ref, entry_state_ref), refs = refs[:8], refs[8:]
    if second:
        (out_ref, grad_out_ref), refs = refs[:2], refs[2:]
    else:
        (grad_out_ref,), refs = refs[:1], refs[1:]
    (da0, da1, db0, db1, do0, do1, part_ref, sums_ref, states_sums_ref), refs = refs[:9], refs[9:]
    (acc_a0, acc_a1, acc_b0, acc_b1, acc_o0, acc_o1, dstate, next_state, conv_edge, states_edge, gain, sums, states_sums) = refs
    step = pl.program_id(0)
    half = gate_ref.shape[1] // 2
    units = 2 * half

    @pl.when(step == 0)
    def _():
        for ref in (acc_a0, acc_a1, acc_b0, acc_b1, acc_o0, acc_o1, dstate, next_state, conv_edge, states_edge, sums, states_sums):
            ref[...] = jnp.zeros_like(ref)
        gain[0:1, :] = gain_row(b0[...])

    marks = marks_ref[...]
    hidden = h_ref[...].astype(f32)
    branch, total, inverse = branch_of(own_ref, other_ref, units)
    if second:
        produced = hidden + branch
        out_ref[...] = produced.astype(bf16)
        grad_out = marks[:, 9:10] * (produced - target_ref[...])
        grad_out_ref[...] = grad_out
    else:
        next_gain = next_gain_ref[0:1, :]
        grad_normed = grad_own_ref[...].astype(f32) + grad_other_ref[...].astype(f32)
        grad_out, gain_term = norm_backward(grad_normed, next_h_ref[...].astype(f32), next_out_ref[...], next_gain)
        sums[7:8, :] += jnp.sum(gain_term, axis=0, keepdims=True)
        grad_out_ref[...] = grad_out
    grad = grad_out.astype(bf16)
    inner = jnp.sum(grad.astype(f32) * total, axis=1, keepdims=True) * (inverse * inverse * inverse) / (2 * units)
    taps = small_ref[...]
    gate = gate_ref[...]
    y = y_ref[...]
    gate_sig = jax.nn.sigmoid(gate)
    gate_silu = gate * gate_sig
    gated = y * gate_silu
    gated_unit = gated * inverse
    grad_mixed = jnp.concatenate([nn(grad, o0[...]), nn(grad, o1[...])], axis=1)
    mixed = (gated_unit * taps[5:6]).astype(bf16)
    acc_o0[...] += tn(grad, mixed[:, :half])
    acc_o1[...] += tn(grad, mixed[:, half:])
    sums[5:6, :] += jnp.sum(grad_mixed * gated_unit, axis=0, keepdims=True)
    grad_gated = grad_mixed * taps[5:6] * inverse - gated * inner
    grad_gate = grad_gated * y * (gate_sig * (1.0 + gate * (1.0 - gate_sig)))
    grad_y_low = (grad_gated * gate_silu).astype(bf16)
    grad_y = grad_y_low.astype(f32)

    conved = conv_ref[...]
    value_sig = jax.nn.sigmoid(conved)
    values = conved * value_sig
    conved_states = conv_states_ref[...]
    states_sig = jax.nn.sigmoid(conved_states)
    states_in = conved_states * states_sig
    b_rows = states_in[:, :STATE].astype(bf16)
    c_rows = states_in[:, STATE:].astype(bf16)
    shifted, steps, log_steps, logs, entry, tail, through, row, column = decay_parts(steps_ref[...], head_ref[...], marks, heads)
    spreader = spread_ref[...]
    spread_steps = spread(steps, spreader)
    spread_entry = spread(entry, spreader)
    spread_tail = spread(tail, spreader)
    through_row = spread(jnp.broadcast_to(through, (8, LANES)), spreader)[0:1]
    scaled_low = (values * spread_steps).astype(bf16)
    scaled = scaled_low.astype(f32)
    mask = linked_mask(row, column, marks, segment_ref[...])
    scores = nt(c_rows, b_rows)
    logs_across = jnp.transpose(logs)
    lane = lax.broadcasted_iota(jnp.int32, (1, LANES), 1)
    grad_scores = jnp.zeros((SPAN, SPAN), f32)
    pieces = []
    zero = jnp.zeros((), bf16)
    for pair in range(heads // 2):
        block = scaled_low[:, pair * LANES : (pair + 1) * LANES]
        grad_block = grad_y_low[:, pair * LANES : (pair + 1) * LANES]
        grad_left = jnp.where(lane < HEAD_DIM, grad_block, zero)
        grad_right = jnp.where(lane < HEAD_DIM, zero, grad_block)
        mixes = []
        for head, grad_one in ((2 * pair, grad_left), (2 * pair + 1, grad_right)):
            factor = jnp.exp(logs[:, head : head + 1] - logs_across[head : head + 1, :] + mask)
            mixes.append((factor * scores).astype(bf16))
            grad_scores = grad_scores + nt(grad_one, block) * factor
        pieces.append(tn(jnp.concatenate(mixes, axis=0), jnp.concatenate([grad_left, grad_right], axis=0)))
    held = entry_state_ref[0]
    held_low = held.astype(bf16)
    gradient = dstate[...]
    gradient_low = gradient.astype(bf16)
    grad_scaled = jnp.concatenate(pieces, axis=1) + spread_tail * nn(b_rows, gradient_low)
    grad_entry = (spread_entry * grad_y).astype(bf16)
    grad_scores_low = grad_scores.astype(bf16)
    grad_c = nn(grad_scores_low, b_rows) + nt(grad_entry, held_low)
    grad_b = tn(grad_scores_low, c_rows) + nt((spread_tail * scaled).astype(bf16), gradient_low)
    state_term = jnp.sum(gradient * next_state[...], axis=0, keepdims=True)
    dstate[...] = through_row * gradient + tn(c_rows, grad_entry)
    next_state[...] = held
    skip = taps[6:7]
    sums[6:7, :] += jnp.sum(grad_y * values, axis=0, keepdims=True)
    grad_logs = gathered_heads(grad_y * (y - skip * values) - scaled * grad_scaled, spreader)
    state_heads = gathered_heads(jnp.broadcast_to(state_term, (8, units)), spreader)[0:1]
    last_row = lax.broadcasted_iota(jnp.int32, (SPAN, 1), 0) == SPAN - 1
    grad_logs = grad_logs + jnp.where(last_row, state_heads, 0.0)
    upper = (row <= column).astype(bf16)
    grad_log_steps = running_sum(upper, grad_logs)
    grad_steps = gathered_heads(grad_scaled * values, spreader) - head_ref[1:2, :LANES] * grad_log_steps
    grad_steps_in = jnp.where(lane < heads, grad_steps * jax.nn.sigmoid(shifted), 0.0)
    states_sums[5:6, :] += jnp.concatenate(
        [
            jnp.sum(grad_steps_in, axis=0, keepdims=True),
            jnp.sum(grad_log_steps * log_steps, axis=0, keepdims=True),
        ],
        axis=1,
    )
    grad_values = grad_scaled * spread_steps + skip * grad_y
    grad_conved = grad_values * (value_sig * (1.0 + conved * (1.0 - value_sig)))
    grad_states = jnp.concatenate([grad_b, grad_c], axis=1)
    grad_conved_states = grad_states * (states_sig * (1.0 + conved_states * (1.0 - states_sig)))

    def conv_backward(block, edge, tap_rows, raw, total_ref):
        result = tap_rows[3:4] * block
        total_ref[3:4, :] += jnp.sum(block * raw, axis=0, keepdims=True)
        total_ref[4:5, :] += jnp.sum(block, axis=0, keepdims=True)
        for lag in (1, 2, 3):
            term = moved_up(block, edge, lag) * marks[:, 5 + lag : 6 + lag]
            result = result + tap_rows[3 - lag : 4 - lag] * term
            total_ref[3 - lag : 4 - lag, :] += jnp.sum(term * raw, axis=0, keepdims=True)
        return result

    grad_raw = conv_backward(grad_conved, conv_edge[...], taps, raw_ref[...], sums).astype(bf16)
    grad_raw_states = conv_backward(
        grad_conved_states, states_edge[...], states_small_ref[...], raw_states_ref[...], states_sums
    )
    conv_edge[...] = grad_conved[:8]
    states_edge[...] = grad_conved_states[:8]
    grad_gate = grad_gate.astype(bf16)
    scale = lax.rsqrt(jnp.mean(hidden * hidden, axis=1, keepdims=True) + epsilon)
    normed = (hidden * scale * gain[0:1, :]).astype(bf16)
    turned = marks[0:1, 10:11] > 0.5
    first_states = jnp.where(turned, grad_raw_states[:, STATE:], grad_raw_states[:, :STATE])
    second_states = jnp.where(turned, grad_raw_states[:, :STATE], grad_raw_states[:, STATE:])
    grad_a0 = jnp.concatenate([grad_gate[:, :half], first_states.astype(bf16)], axis=1)
    grad_a1 = jnp.concatenate([grad_gate[:, half:], second_states.astype(bf16)], axis=1)
    own_steps = jnp.where(lane < heads // 2, grad_steps_in, 0.0)
    other_steps = pltpu.roll(grad_steps_in, LANES - heads // 2, 1)
    other_steps = jnp.where(lane < heads // 2, other_steps, 0.0)
    grad_b0 = jnp.concatenate([grad_raw[:, :half], own_steps.astype(bf16)], axis=1)
    grad_b1 = jnp.concatenate([grad_raw[:, half:], other_steps.astype(bf16)], axis=1)
    acc_a0[...] += tn(normed, grad_a0)
    acc_a1[...] += tn(normed, grad_a1)
    acc_b0[...] += tn(normed, grad_b0)
    acc_b1[...] += tn(normed, grad_b1)
    part = nt(grad_a0, a0[...]) + nt(grad_a1, a1[...]) + nt(grad_b0, b0[...]) + nt(grad_b1, b1[...])
    part_ref[...] = part.astype(bf16)

    @pl.when(step == pl.num_programs(0) - 1)
    def _():
        for out, acc in ((da0, acc_a0), (da1, acc_a1), (db0, acc_b0), (db1, acc_b1), (do0, acc_o0), (do1, acc_o1)):
            out[...] = acc[...].astype(out.dtype)
        sums_ref[...] = sums[...]
        states_sums_ref[...] = states_sums[...]


def norm_backward(grad_normed, hidden, grad_out, gain):
    scale = lax.rsqrt(jnp.mean(hidden * hidden, axis=1, keepdims=True) + epsilon)
    weighted = grad_normed * gain
    shared = jnp.mean(weighted * hidden, axis=1, keepdims=True) * (scale * scale * scale)
    return grad_out + scale * weighted - hidden * shared, grad_normed * hidden * scale


VMEM_LIMIT = 60 * 1024 * 1024


def spreader_of(units):
    one = (np.arange(LANES)[:, None] == np.arange(units)[None, :] // HEAD_DIM).astype(np.float32)
    return jnp.asarray(np.concatenate([one, one], axis=0), bf16)


def rows_spec(width, last=None):
    if last is None:
        return pl.BlockSpec((SPAN, width), lambda i: (i, 0))
    return pl.BlockSpec((SPAN, width), lambda i: (last - i, 0))


def whole_spec(array):
    return pl.BlockSpec(array.shape, lambda i: (0,) * array.ndim)


def common_args(weights, marks, segment_row, params, chunks, reverse):
    last = chunks - 1
    spreader = spreader_of(params[0].shape[1])
    arrays = list(weights) + [marks, segment_row] + list(params) + [spreader]
    specs = [whole_spec(w) for w in weights]
    specs.append(rows_spec(LANES, last if reverse else None))
    specs.append(pl.BlockSpec((1, SPAN), (lambda i: (0, last - i)) if reverse else (lambda i: (0, i))))
    specs += [whole_spec(p) for p in params] + [whole_spec(spreader)]
    return arrays, specs


def forward_layer(h, parts, weights, marks, segment_row, params):
    length, width = h.shape
    units = params[0].shape[1]
    heads = units // HEAD_DIM
    chunks = length // SPAN
    second = parts is not None
    shared, shared_specs = common_args(weights, marks, segment_row, params, chunks, False)
    inputs, specs = [h], [rows_spec(width)]
    outs, out_specs = [], []
    if second:
        inputs += list(parts)
        specs += [rows_spec(width + LANES)] * 2
        outs.append(jax.ShapeDtypeStruct((length, width), bf16))
        out_specs.append(rows_spec(width))
    for columns in (units, units, units, units, 2 * STATE, 2 * STATE, LANES):
        outs.append(jax.ShapeDtypeStruct((length, columns), f32))
        out_specs.append(rows_spec(columns))
    outs.append(jax.ShapeDtypeStruct((chunks, STATE, units), f32))
    out_specs.append(pl.BlockSpec((1, STATE, units), lambda i: (i, 0, 0)))
    outs.append(jax.ShapeDtypeStruct((length, width + LANES), bf16))
    out_specs.append(rows_spec(width + LANES))
    results = pl.pallas_call(
        functools.partial(forward_kernel, second, heads),
        grid=(chunks,),
        in_specs=specs + shared_specs,
        out_specs=out_specs,
        out_shape=outs,
        scratch_shapes=[
            pltpu.VMEM((STATE, units), f32),
            pltpu.VMEM((8, units), f32),
            pltpu.VMEM((8, 2 * STATE), f32),
            pltpu.VMEM((8, width), f32),
        ],
        compiler_params=pltpu.CompilerParams(vmem_limit_bytes=VMEM_LIMIT, dimension_semantics=("arbitrary",)),
        cost_estimate=pl.CostEstimate(flops=6_000_000_000, bytes_accessed=30_000_000, transcendentals=6_000_000),
    )(*inputs, *shared)
    if second:
        return results[0], results[1:9], results[9]
    return h, results[:8], results[8]


def backward_layer(h, parts, extra, weights, marks, segment_row, params, saved):
    length, width = h.shape
    units = params[0].shape[1]
    heads = units // HEAD_DIM
    chunks = length // SPAN
    last = chunks - 1
    second = len(extra) == 1
    shared, shared_specs = common_args(weights, marks, segment_row, params, chunks, True)
    inputs = [h] + list(parts) + list(extra)
    specs = [rows_spec(width, last)] + [rows_spec(width + LANES, last)] * 2
    if second:
        specs += [rows_spec(width, last)]
    else:
        specs += [rows_spec(width, last)] * 4 + [whole_spec(extra[4])]
    saved_specs = [rows_spec(s.shape[1], last) for s in saved[:7]]
    saved_specs.append(pl.BlockSpec((1, STATE, units), lambda i: (last - i, 0, 0)))
    outs, out_specs = [], []
    if second:
        outs.append(jax.ShapeDtypeStruct((length, width), bf16))
        out_specs.append(rows_spec(width, last))
    outs.append(jax.ShapeDtypeStruct((length, width), f32))
    out_specs.append(rows_spec(width, last))
    for w in weights:
        outs.append(jax.ShapeDtypeStruct(w.shape, bf16))
        out_specs.append(whole_spec(w))
    outs.append(jax.ShapeDtypeStruct((length, width), bf16))
    out_specs.append(rows_spec(width, last))
    for columns in (units, 2 * STATE):
        outs.append(jax.ShapeDtypeStruct((8, columns), f32))
        out_specs.append(pl.BlockSpec((8, columns), lambda i: (0, 0)))
    return pl.pallas_call(
        functools.partial(backward_kernel, second, heads),
        grid=(chunks,),
        in_specs=specs + shared_specs + saved_specs,
        out_specs=out_specs,
        out_shape=outs,
        scratch_shapes=[pltpu.VMEM(w.shape, f32) for w in weights]
        + [
            pltpu.VMEM((STATE, units), f32),
            pltpu.VMEM((STATE, units), f32),
            pltpu.VMEM((8, units), f32),
            pltpu.VMEM((8, 2 * STATE), f32),
            pltpu.VMEM((8, width), f32),
            pltpu.VMEM((8, units), f32),
            pltpu.VMEM((8, 2 * STATE), f32),
        ],
        compiler_params=pltpu.CompilerParams(vmem_limit_bytes=VMEM_LIMIT, dimension_semantics=("arbitrary",)),
        cost_estimate=pl.CostEstimate(flops=20_000_000_000, bytes_accessed=50_000_000, transcendentals=9_000_000),
    )(*inputs, *shared, *saved)


def token_marks(segment, counted, turned):
    length = segment.shape[0]
    blocks = segment.reshape(-1, SPAN)
    ends = blocks[:, -1]
    before = jnp.concatenate([jnp.full((1,), -1, segment.dtype), ends[:-1]])
    columns = [jnp.pad(segment, (lag, 0), constant_values=-1)[:length] == segment for lag in (1, 2, 3)]
    columns += [(blocks == before[:, None]).reshape(-1), (blocks == ends[:, None]).reshape(-1), segment]
    columns += [jnp.pad(segment, (0, lag), constant_values=-1)[lag:] == segment for lag in (1, 2, 3)]
    columns += [counted, jnp.broadcast_to(turned, segment.shape)]
    stacked = jnp.stack([c.astype(f32) for c in columns], axis=1)
    return jnp.pad(stacked, ((0, 0), (0, LANES - stacked.shape[1])))


def factors_of(number):
    found = []
    while number > 1:
        size = 2 if number % 4 or not found else 4
        size = size if number % size == 0 else number
        found.append(size)
        number //= size
    return found[::-1] or [1]


def digit_pairs(size, stride, total, moves):
    pairs = []
    for index in range(total):
        place = index // stride % size
        for start, end in moves:
            if start == place:
                pairs.append((index, index + (end - start) * stride))
    return pairs


class Line:
    def __init__(self, size, stride, total):
        self.size, self.stride, self.total = size, stride, total

    def place(self):
        return lax.axis_index("dp") // self.stride % self.size

    def send(self, block, moves):
        return lax.ppermute(block, "dp", digit_pairs(self.size, self.stride, self.total, moves))

    def gather(self, block):
        size, place = self.size, self.place()
        if size == 1:
            return block[None]
        if size == 2:
            other = self.send(block, [(0, 1), (1, 0)])
            first = place == 0
            return jnp.stack([jnp.where(first, block, other), jnp.where(first, other, block)])
        ups, downs = [], []
        up = down = block
        for hop in range(1, size):
            up = self.send(up, [(p, p + 1) for p in range(size - 1) if p >= hop - 1])
            down = self.send(down, [(p, p - 1) for p in range(1, size) if p <= size - hop])
            ups.append(up)
            downs.append(down)
        row = jnp.stack(ups[::-1] + [block] + downs)
        return lax.dynamic_slice_in_dim(row, size - 1 - place, size, 0)

    def reduce(self, blocks):
        size, place = self.size, self.place()
        if size == 1:
            return blocks[0]
        at = lambda index: lax.dynamic_index_in_dim(blocks, jnp.clip(index, 0, size - 1), 0, keepdims=False).astype(f32)
        own = at(place)
        if size == 2:
            other = self.send(at(1 - place).astype(bf16), [(0, 1), (1, 0)])
            return (own + other.astype(f32)).astype(bf16)
        up = down = None
        for far in range(size - 1, 0, -1):
            up_block, down_block = at(place + far), at(place - far)
            if up is not None:
                up_block, down_block = up_block + up.astype(f32), down_block + down.astype(f32)
            up = self.send(up_block.astype(bf16), [(p, p + 1) for p in range(size - far)])
            down = self.send(down_block.astype(bf16), [(p, p - 1) for p in range(far, size)])
        return (own + up.astype(f32) + down.astype(f32)).astype(bf16)

    def total_of(self, block):
        size = self.size
        if size == 1:
            return block
        if size == 2:
            return block + self.send(block, [(0, 1), (1, 0)])
        result = up = block
        down = block
        for hop in range(1, size):
            up = self.send(up, [(p, p + 1) for p in range(size - 1) if p >= hop - 1])
            down = self.send(down, [(p, p - 1) for p in range(1, size) if p <= size - hop])
            result = result + up + down
        return result


def swapped(block, axis):
    return lax.ppermute(block, axis, [(0, 1), (1, 0)])


def chosen_swap(block, section):
    size = lax.axis_size("tensor")
    pairs = [(section * size + i, section * size + 1 - i) for i in range(size)]
    return lax.ppermute(block, ("section", "tensor"), pairs)


def body(
    x_input,
    teacher,
    segment_ids,
    valid_len,
    norm_gain,
    w_zx,
    w_bc,
    w_dt,
    conv_x,
    conv_bc,
    dt_bias,
    a_log,
    d_skip,
    gnorm_gain,
    w_out,
):
    micro, local_rows, width = x_input.shape
    seq_length = segment_ids.shape[2]
    ranks = lax.axis_size("dp")
    core = lax.axis_index("section")
    turn = lax.axis_index("tensor")
    rank = lax.axis_index("dp")
    on_first = core == 0
    block_rows = w_zx.shape[1]
    half = w_zx.shape[3] // 2
    heads_half = w_dt.shape[2] // 2
    sizes = factors_of(ranks)
    lines = []
    stride = ranks
    for size in sizes:
        stride //= size
        lines.append(Line(size, stride, ranks))

    def pick(pair, index):
        return lax.dynamic_index_in_dim(pair, index, 0, keepdims=False)

    def by_layer(kept, received):
        return jnp.where(on_first, kept, received), jnp.where(on_first, received, kept)

    bc_half = lax.dynamic_slice_in_dim(w_bc[0], turn * STATE, STATE, 1)
    gain_column = jnp.pad(norm_gain[0][:, None], ((0, 0), (LANES // 2, LANES // 2 - 1)))

    def in_pack(part):
        steps = w_dt[0][:, part * heads_half : (part + 1) * heads_half]
        steps = jnp.pad(steps, ((0, 0), (0, LANES - heads_half))) + gain_column
        columns = slice(part * half, (part + 1) * half)
        return jnp.concatenate([w_zx[0][:, 0, columns], bc_half, w_zx[0][:, 1, columns], steps], axis=1)

    in_packs = jnp.stack([in_pack(0), in_pack(1)])
    in_layers = by_layer(pick(in_packs, core), swapped(pick(in_packs, 1 - core), "section"))
    out_packs = jnp.transpose(w_out[0].reshape(2, half, block_rows), (0, 2, 1))
    out_layers = by_layer(pick(out_packs, core), swapped(pick(out_packs, 1 - core), "section"))

    def lines_over(block, chosen):
        for line in reversed(chosen):
            block = line.gather(block)
        return block

    def gathered_in(block):
        first = lines[0].gather(block)
        columns = half + STATE
        rest = lines[1:]
        a_rows = lines_over(first[..., :columns], rest)
        b_part = first[..., columns:]
        b_both = lines_over(jnp.stack([b_part, swapped(b_part, "tensor")]), rest)
        a_rows = jnp.moveaxis(a_rows, len(rest), 0).reshape(width, columns)
        b_both = jnp.moveaxis(b_both, (len(rest), len(rest) + 1), (0, 1)).reshape(2, width, half + LANES)
        return a_rows, swapped(a_rows, "tensor"), b_both[0], b_both[1]

    def gathered_out(block):
        rows = lines_over(lines[0].gather(block), lines[1:])
        rows = jnp.moveaxis(rows, len(lines) - 1, 0).reshape(width, half)
        return rows, swapped(rows, "tensor")

    def whole_rows(rows):
        quarter = local_rows // 2
        own = pick(rows, turn)
        away = lax.dynamic_slice_in_dim(pick(rows, 1 - turn), core * quarter, quarter, 0)
        here = swapped(away, "tensor")
        beside = swapped(here, "section")
        first, second = jnp.where(on_first, here, beside), jnp.where(on_first, beside, here)
        other = jnp.concatenate([first, second], axis=0)
        return jnp.where(turn == 0, jnp.concatenate([own, other]), jnp.concatenate([other, own]))

    x_rows = whole_rows(x_input)
    target = whole_rows(teacher)
    segment = pick(segment_ids[:, 0], turn)
    length = pick(pick(valid_len, turn), rank)
    loss_weight = micro * seq_length * ranks / jnp.sum(valid_len).astype(f32)
    counted = jnp.where(jnp.arange(seq_length) < length, 2.0 * loss_weight, 0.0)
    marks = token_marks(segment, counted, turn)
    segment_row = segment.astype(f32)[None]

    channels = jnp.concatenate([conv_x[0].astype(f32), gnorm_gain.astype(f32)], axis=0)
    channels = jnp.stack([channels[:, :half], channels[:, half:]])
    channels = jnp.stack(by_layer(pick(channels, core), swapped(pick(channels, 1 - core), "section")))
    channels = jnp.concatenate([channels, swapped(channels, "tensor")], axis=2)
    shared = jnp.concatenate(
        [conv_bc[0].astype(f32), jnp.pad(jnp.concatenate([dt_bias, a_log, d_skip]), ((0, 0), (0, 2 * STATE - dt_bias.shape[1])))]
    )
    shared = jnp.stack(by_layer(shared, swapped(shared, "section")))

    def own_heads(row):
        starts = turn * 2 * heads_half + core * heads_half, (1 - turn) * 2 * heads_half + core * heads_half
        return jnp.concatenate([lax.dynamic_slice_in_dim(row, start, heads_half) for start in starts])

    def params_of(layer):
        skips = jnp.repeat(own_heads(shared[layer, 7]), HEAD_DIM)
        small = jnp.concatenate([channels[layer], skips[None], jnp.zeros_like(skips)[None]])
        states_small = jnp.pad(shared[layer, :5], ((0, 3), (0, 0)))
        head_rows = jnp.stack([own_heads(shared[layer, 5]), jnp.exp(own_heads(shared[layer, 6]))])
        head_rows = jnp.pad(head_rows, ((0, 6), (0, LANES - head_rows.shape[1])))
        return small, states_small, head_rows

    params = [params_of(0), params_of(1)]
    weights = [gathered_in(in_layers[0]) + gathered_out(out_layers[0])]
    weights.append(gathered_in(in_layers[1]) + gathered_out(out_layers[1]))

    _, saved_first, part = forward_layer(x_rows, None, weights[0], marks, segment_row, params[0])
    parts_first = (part, swapped(part, "section"))
    hidden, saved_second, part = forward_layer(x_rows, parts_first, weights[1], marks, segment_row, params[1])
    parts_second = (part, swapped(part, "section"))

    results = backward_layer(hidden, parts_second, (target,), weights[1], marks, segment_row, params[1], saved_second)
    produced, grad_out = results[:2]
    grads_second = results[2:8]
    sums_second = results[9:]
    gain_next = jnp.broadcast_to(weights[1][2][:, half + LANES // 2].astype(f32)[None], (8, width))
    extra = (hidden, grad_out, results[8], swapped(results[8], "section"), gain_next)
    results = backward_layer(x_rows, parts_first, extra, weights[0], marks, segment_row, params[0], saved_first)
    grad_hidden = results[0]
    grads_first = results[1:7]
    sums_first = results[8:]
    gain_first = weights[0][2][:, half + LANES // 2].astype(f32)[None]
    grad_normed = results[7].astype(f32) + swapped(results[7], "section").astype(f32)
    grad_out_low = grad_hidden.astype(bf16).astype(f32)
    grad_x, gain_term = norm_backward(grad_normed, x_rows.astype(f32), grad_out_low, gain_first)
    grad_gain_first = jnp.sum(gain_term, axis=0)

    def halves(rows):
        own = lax.dynamic_slice_in_dim(rows, turn * local_rows, local_rows, 0)
        away = lax.dynamic_slice_in_dim(rows, (1 - turn) * local_rows, local_rows, 0)
        return own, away

    def placed(own, received):
        return jnp.where(turn == 0, jnp.stack([own, received]), jnp.stack([received, own]))

    own, away = halves(jnp.where(on_first, hidden, produced))
    layer_outputs = placed(own, swapped(away, "tensor"))
    own_second, away = halves(grad_hidden)
    received_second = chosen_swap(away.astype(bf16), 1)
    own_first, away = halves(grad_x)
    received_first = chosen_swap(away.astype(bf16), 0)
    boundary = placed(
        jnp.where(on_first, own_first, own_second),
        jnp.where(on_first, received_first, received_second).astype(f32),
    )

    def add(left, right):
        return (left.astype(f32) + right.astype(f32)).astype(bf16)

    def reduced(grads):
        a_own, a_other, b_own, b_other, o_own, o_other = grads
        shape = tuple(sizes) + (block_rows,)

        def over_rest(block):
            lead = block.shape[0]
            for line in reversed(lines[1:]):
                index = lines.index(line) + 1
                block = line.reduce(jnp.moveaxis(block, index, 0))
            return block

        a_sum = add(a_own, swapped(a_other, "tensor")).reshape((1,) + shape + (-1,))
        a_sum = over_rest(a_sum)[0]
        b_sum = over_rest(jnp.stack([b_own, b_other]).reshape((2,) + shape + (-1,)))
        b_sum = add(b_sum[0], swapped(b_sum[1], "tensor"))
        o_sum = over_rest(add(o_own, swapped(o_other, "tensor")).reshape((1,) + shape + (-1,)))[0]
        return lines[0].reduce(jnp.concatenate([a_sum, b_sum, o_sum], axis=-1))

    owned_second = reduced(grads_second)
    owned_first = reduced(grads_first)
    mine, others = by_layer(owned_first, owned_second)
    beside = swapped(others, "section").astype(f32)
    mine = mine.astype(f32)

    def both(columns):
        start, size = columns
        here, there = mine[:, start : start + size], beside[:, start : start + size]
        return jnp.where(on_first, jnp.concatenate([here, there], 1), jnp.concatenate([there, here], 1))

    b_start = half + STATE
    o_start = b_start + half + LANES
    grad_zx = jnp.stack([both((0, half)), both((b_start, half))], axis=1)
    bc_own = mine[:, half:b_start] + beside[:, half:b_start]
    bc_other = swapped(bc_own, "tensor")
    grad_bc = jnp.where(turn == 0, jnp.concatenate([bc_own, bc_other], 1), jnp.concatenate([bc_other, bc_own], 1))
    grad_dt = both((b_start + half, heads_half))
    grad_out_w = jnp.transpose(both((o_start, half)))

    def split_pack(sums, states_sums):
        skips = jnp.sum(sums[6].reshape(2 * heads_half, HEAD_DIM), axis=1)
        heads = jnp.stack([skips, states_sums[5, : 2 * heads_half], states_sums[5, STATE : STATE + 2 * heads_half]])
        heads = heads.reshape(3, 2, heads_half)
        heads = jnp.pad(heads, ((0, 0), (0, 0), (0, half - heads_half))).reshape(3, 2 * half)
        return jnp.concatenate([sums[:6], heads], axis=0)

    split_first, split_second = split_pack(*sums_first), split_pack(*sums_second)
    mine, others = by_layer(split_first, split_second)
    beside = swapped(others, "section")
    packed = jnp.concatenate([mine, beside])
    packed = packed[:, :half] + swapped(packed[:, half:], "tensor")
    mine, others = by_layer(sums_first[1][:5], sums_second[1][:5])
    states_total = mine + swapped(others, "section")
    gain_total = jnp.where(on_first, grad_gain_first, sums_first[0][7])
    total = jnp.concatenate([states_total.reshape(-1), gain_total]).reshape(-1, 2 * STATE)
    total = total + swapped(total, "tensor")
    for line in lines:
        packed = line.total_of(packed)
        total = line.total_of(total)
    rows = packed.shape[0] // 2
    here, there = packed[:rows], packed[rows:]

    def in_order(here, there):
        return jnp.where(on_first, jnp.concatenate([here, there], -1), jnp.concatenate([there, here], -1))

    channel_grads = in_order(here[:6], there[:6])
    head_grads = in_order(here[6:9, :heads_half], there[6:9, :heads_half])
    states_total = total[:5]
    gain_total = lax.dynamic_slice_in_dim(total[5:].reshape(-1), rank * block_rows, block_rows)
    return (
        layer_outputs[None],
        boundary[None],
        gain_total[None],
        grad_zx[None],
        grad_bc[None],
        grad_dt[None],
        channel_grads[None, :5],
        states_total[None],
        head_grads[1][None],
        head_grads[2][None],
        head_grads[0][None],
        channel_grads[5][None],
        grad_out_w[None],
    )


def solution(mesh):
    placed = (
        P(None, ("dp", "tensor"), None),
        P(None, ("dp", "tensor"), None),
        P(None, "dp", None),
        P(),
        P("section", "dp"),
        P("section", "dp", None, "tensor"),
        P("section", "dp", None),
        P("section", "dp", "tensor"),
        P("section", None, "tensor"),
        P("section", None, None),
        P("section", None),
        P("section", None),
        P("section", None),
        P("section", "tensor"),
        P("section", "tensor", "dp"),
    )
    return jax.shard_map(
        body,
        mesh=mesh,
        in_specs=placed,
        out_specs=(
            P("section", None, ("dp", "tensor"), None),
            P("section", None, ("dp", "tensor"), None),
            P("section", "dp"),
            P("section", "dp", None, "tensor"),
            P("section", "dp", None),
            P("section", "dp", "tensor"),
            P("section", None, "tensor"),
            P("section", None, None),
            P("section", "tensor"),
            P("section", "tensor"),
            P("section", "tensor"),
            P("section", "tensor"),
            P("section", "tensor", "dp"),
        ),
        check_vma=False,
    )
```

time: 2490 us -> 605 us (0.24)
  matrix products: 572 us -> 0 us
  local copies, waits for them, and re-layouts: 574 us -> 61.7 us
  other arithmetic: 516 us -> 74.7 us
  waiting for transfers between devices: 568 us -> 201 us
  blocking collectives: 169 us -> 0 us
  Pallas kernels: 0 us -> 131 us
  starting transfers between devices: 8.27 us -> 126 us
  loops' own time: 32.1 us -> 0 us
    dot_general x105 -> x0, matrix products: 572 us -> none  [the longest x12 203 us: block_scan(): jnp.einsum('chij,cjhp->cihp', factors * scores[:, None], scaled, precisio...]
    unnamed x24 -> x0, waiting for transfers between devices: 299 us -> none
    ppermute x4 -> x96, waiting for transfers between devices: 6.13 us -> 201 us  [the longest x62 115 us: send(): lax.ppermute(block, 'dp', digit_pairs(self.size, self.stride, self.total,...]
    mul x116 -> x1, other arithmetic: 152 us -> 0.01 us  [norm_backward(): jnp.mean(weighted * hidden, axis=1, keepdims=True) * (scale * scale * scale)]
    reduce_sum x58 -> x5, other arithmetic: 138 us -> 7.08 us  [the longest x1 3.34 us: body(): grad_gain_first = jnp.sum(gain_term, axis=0)]
    pallas_call x0 -> x4, Pallas kernels: none -> 131 us  [the longest x2 86.6 us: backward_layer(): pl.pallas_call(functools.partial(backward_kernel, second, heads), grid=(c...]
    all_gather x11 -> x0, waiting for transfers between devices: 129 us -> none  [the longest x9 129 us: gather_rows(): return lax.all_gather(rows_here, 'tensor', axis=0, tiled=True)]
    ppermute x4 -> x96, starting transfers between devices: 6.66 us -> 126 us  [the longest x62 98.5 us: send(): lax.ppermute(block, 'dp', digit_pairs(self.size, self.stride, self.total,...]
  transfers between devices with their start and end apart: 25 -> 96, of which waited for: 17 -> 35; matrix products, arithmetic and copies ran while one was open for 24% -> 20% of each run, Pallas kernels for 0% -> 15%
where the time goes in v1:
time: 605 us; the launch traced here: 597 us
  waiting for transfers between devices  201 us (33%)
  Pallas kernels  131 us (22%)
  starting transfers between devices  126 us (21%)
  other arithmetic  74.7 us (12%)
  local copies, waits for them, and re-layouts  61.7 us (10%)
    ppermute x62, waiting for transfers between devices, send(): lax.ppermute(block, 'dp', digit_pairs(self.size, self.stride, self.total,...  115 us
    ppermute x62, starting transfers between devices, send(): lax.ppermute(block, 'dp', digit_pairs(self.size, self.stride, self.total,...  98.5 us
    pallas_call x2, Pallas kernels, backward_layer(): pl.pallas_call(functools.partial(backward_kernel, second, heads), grid=(c...  86.6 us
    ppermute x32, waiting for transfers between devices, swapped(): return lax.ppermute(block, axis, [(0, 1), (1, 0)])  78.4 us
    pallas_call x2, Pallas kernels, forward_layer(): pl.pallas_call(functools.partial(forward_kernel, second, heads), grid=(ch...  44.1 us
    ppermute x32, starting transfers between devices, swapped(): return lax.ppermute(block, axis, [(0, 1), (1, 0)])  23.5 us
  transfers between devices with their start and end apart: 96, of which 35 were waited for; matrix products, arithmetic and copies ran while one was open for 20% of the time, Pallas kernels for 15%

profile of v1, /device:TPU:0, one launch (start us, length us, event | category | flops | bytes accessed | tf_op | source)
XLA Modules:
  0.0 597.2 jit_solution(11169074341011802383)
XLA Ops:
  18.9 3.0 collective-permute-start
  29.5 2.1 dynamic-slice_bitcast_fusion.3
  41.2 2.7 stack.378
  62.3 4.0 collective-permute-start.36
  66.3 3.5 collective-permute-start.14
  76.8 3.0 collective-permute-done.39
  85.0 8.1 %collective-permute-start.26 = (bf16[96,1024]{1,0:T(8,128)(2,1)S(1)}, bf16[96,1024]{1,0:T(8,128)(2,1)S(1)}, u32[]{:S(2)}, u32[]{:S(2)}) collective-permute-start(bf16[96,1024]{1,0:T(8,128)(2,1)S(1)} %get-tuple-element.192), channel_id=1, source_target_pairs={{0,4},{2,6},{4,8},{6,10},{8,12},{10,14},{1,5},{3,7},{5,9},{7,11},{... | collective-permute-start | bytes 589832 | tf_op jit(solution)/shard_map/ppermute | solution.py:546
  93.3 6.4 %collective-permute-start.3 = (bf16[96,1024]{1,0:T(8,128)(2,1)S(1)}, bf16[96,1024]{1,0:T(8,128)(2,1)S(1)}, u32[]{:S(2)}, u32[]{:S(2)}) collective-permute-start(bf16[96,1024]{1,0:T(8,128)(2,1)S(1)} %get-tuple-element.193), channel_id=1, source_target_pairs={{0,4},{2,6},{4,8},{6,10},{8,12},{10,14},{1,5},{3,7},{5,9},{7,11},{... | collective-permute-start | bytes 589832 | tf_op jit(solution)/shard_map/ppermute | solution.py:546
  101.0 5.6 collective-permute-done.19
  108.0 4.9 collective-permute-done.41
  117.9 2.6 collective-permute-done.20
  125.3 10.2 %collective-permute-done.6 = bf16[96,1024]{1,0:T(8,128)(2,1)S(1)} collective-permute-done((bf16[96,1024]{1,0:T(8,128)(2,1)S(1)}, bf16[96,1024]{1,0:T(8,128)(2,1)S(1)}, u32[]{:S(2)}, u32[]{:S(2)}) %collective-permute-start.6) | collective-permute-done | bytes 196640 | tf_op jit(solution)/shard_map/ppermute | solution.py:546
  138.3 8.1 %collective-permute-done.7 = bf16[96,1024]{1,0:T(8,128)(2,1)S(1)} collective-permute-done((bf16[96,1024]{1,0:T(8,128)(2,1)S(1)}, bf16[96,1024]{1,0:T(8,128)(2,1)S(1)}, u32[]{:S(2)}, u32[]{:S(2)}) %collective-permute-start.7) | collective-permute-done | bytes 196640 | tf_op jit(solution)/shard_map/ppermute | solution.py:546
  147.7 8.2 %collective-permute-done.8 = bf16[96,1024]{1,0:T(8,128)(2,1)S(1)} collective-permute-done((bf16[96,1024]{1,0:T(8,128)(2,1)S(1)}, bf16[96,1024]{1,0:T(8,128)(2,1)S(1)}, u32[]{:S(2)}, u32[]{:S(2)}) %collective-permute-start.8) | collective-permute-done | bytes 196640 | tf_op jit(solution)/shard_map/ppermute | solution.py:546
  157.5 6.0 %collective-permute-done.31 = bf16[96,1024]{1,0:T(8,128)(2,1)S(1)} collective-permute-done((bf16[96,1024]{1,0:T(8,128)(2,1)S(1)}, bf16[96,1024]{1,0:T(8,128)(2,1)S(1)}, u32[]{:S(2)}, u32[]{:S(2)}) %collective-permute-start.31) | collective-permute-done | bytes 196640 | tf_op jit(solution)/shard_map/ppermute | solution.py:546
  166.1 8.0 %collective-permute-done.11 = bf16[4,96,512]{2,1,0:T(8,128)(2,1)S(1)} collective-permute-done((bf16[4,96,512]{2,1,0:T(8,128)(2,1)S(1)}, bf16[4,96,512]{2,1,0:T(8,128)(2,1)S(1)}, u32[]{:S(2)}, u32[]{:S(2)}) %collective-permute-start.11) | collective-permute-done | bytes 393248 | tf_op jit(solution)/shard_map/ppermute | solution.py:600
  174.2 2.2 fusion
  179.2 7.8 %collective-permute-done.12 = bf16[2,4,96,512]{3,2,1,0:T(8,128)(2,1)S(1)} collective-permute-done((bf16[2,4,96,512]{3,2,1,0:T(8,128)(2,1)S(1)}, bf16[2,4,96,512]{3,2,1,0:T(8,128)(2,1)S(1)}, u32[]{:S(2)}, u32[]{:S(2)}) %collective-permute-start.12) | collective-permute-done | bytes 786464 | tf_op jit(solution)/shard_map/ppermute | solution.py:546
  190.1 3.3 collective-permute-done.10.refs_2_.refs_9_
  194.3 21.0 %shard_map.282 = (f32[1024,768]{1,0:T(8,128)}, f32[1024,768]{1,0:T(8,128)}, f32[1024,768]{1,0:T(8,128)}, f32[1024,768]{1,0:T(8,128)}, f32[1024,256]{1,0:T(8,128)...) custom-call(bf16[1024,768]{1,0:T(8,128)(2,1)} %get-tuple-element.157.refs_0_, ...), custom_call_target="tpu_custom_call" | custom-call | flops 6000000000 | bytes 30000000 | tf_op jit(solution)/shard_map/pallas_call | solution.py:434
  220.9 6.5 %collective-permute-done.32 = bf16[4,96,512]{2,1,0:T(8,128)(2,1)S(1)} collective-permute-done((bf16[4,96,512]{2,1,0:T(8,128)(2,1)S(1)}, bf16[4,96,512]{2,1,0:T(8,128)(2,1)S(1)}, u32[]{:S(2)}, u32[]{:S(2)}) %collective-permute-start.32) | collective-permute-done | bytes 393248 | tf_op jit(solution)/shard_map/ppermute | solution.py:546
  229.9 13.9 %collective-permute-done.35 = bf16[2,4,96,512]{3,2,1,0:T(8,128)(2,1)S(1)} collective-permute-done((bf16[2,4,96,512]{3,2,1,0:T(8,128)(2,1)S(1)}, bf16[2,4,96,512]{3,2,1,0:T(8,128)(2,1)S(1)}, u32[]{:S(2)}, u32[]{:S(2)}) %collective-permute-start.35) | collective-permute-done | bytes 786464 | tf_op jit(solution)/shard_map/ppermute | solution.py:546
  247.2 11.9 %collective-permute-done.43.refs_8_.refs_9_ = bf16[768,384]{1,0:T(8,128)(2,1)S(1)} collective-permute-done((bf16[768,384]{1,0:T(8,128)(2,1)S(1)}, bf16[768,384]{1,0:T(8,128)(2,1)S(1)}, u32[]{:S(2)}, u32[]{:S(2)}) %collective-permute-start.43) | collective-permute-done | bytes 589856 | tf_op jit(solution)/shard_map/ppermute | solution.py:600
  260.1 23.1 %shard_map.283 = (bf16[1024,768]{1,0:T(8,128)(2,1)}, f32[1024,768]{1,0:T(8,128)}, f32[1024,768]{1,0:T(8,128)}, f32[1024,768]{1,0:T(8,128)}, f32[1024,768]{1,0:T(...) custom-call(bf16[1024,768]{1,0:T(8,128)(2,1)} %get-tuple-element.157, ...), custom_call_target="tpu_custom_call" | custom-call | flops 6000000000 | bytes 30000000 | tf_op jit(solution)/shard_map/pallas_call | solution.py:434
  284.5 4.0 collective-permute-done.46
  294.4 42.6 %shard_map.284 = (bf16[1024,768]{1,0:T(8,128)(2,1)}, f32[1024,768]{1,0:T(8,128)}, bf16[768,512]{1,0:T(8,128)(2,1)}, bf16[768,512]{1,0:T(8,128)(2,1)}, bf16[768,5...) custom-call(bf16[1024,768]{1,0:T(8,128)(2,1)} %get-tuple-element.54., ...), custom_call_target="tpu_custom_call" | custom-call | flops 20000000000 | bytes 50000000 | tf_op jit(solution)/shard_map/pallas_call | solution.py:484
  344.6 25.8 %collective-permute-done.77 = bf16[768,384]{1,0:T(8,128)(2,1)} collective-permute-done((bf16[768,384]{1,0:T(8,128)(2,1)}, bf16[768,384]{1,0:T(8,128)(2,1)}, u32[]{:S(2)}, u32[]{:S(2)}) %collective-permute-start.77) | collective-permute-done | bytes 589856 | tf_op jit(solution)/shard_map/ppermute | solution.py:600
  378.2 8.9 %collective-permute-done.47 = bf16[512,768]{1,0:T(8,128)(2,1)S(1)} collective-permute-done((bf16[512,768]{1,0:T(8,128)(2,1)S(1)}, bf16[512,768]{1,0:T(8,128)(2,1)S(1)}, u32[]{:S(2)}, u32[]{:S(2)}) %collective-permute-start.47) | collective-permute-done | bytes 786464 | tf_op jit(solution)/shard_map/ppermute | solution.py:600
  388.8 6.0 %collective-permute-done.76 = bf16[4,96,512]{2,1,0:T(8,128)(2,1)S(1)} collective-permute-done((bf16[4,96,512]{2,1,0:T(8,128)(2,1)S(1)}, bf16[4,96,512]{2,1,0:T(8,128)(2,1)S(1)}, u32[]{:S(2)}, u32[]{:S(2)}) %collective-permute-start.76) | collective-permute-done | bytes 393248 | tf_op jit(solution)/shard_map/ppermute | solution.py:600
  395.1 2.3 collective-permute-start.79
  399.3 44.0 %shard_map.285 = (f32[1024,768]{1,0:T(8,128)}, bf16[768,512]{1,0:T(8,128)(2,1)}, bf16[768,512]{1,0:T(8,128)(2,1)}, bf16[768,512]{1,0:T(8,128)(2,1)}, bf16[768,51...) custom-call(bf16[1024,768]{1,0:T(8,128)(2,1)} %get-tuple-element.157, ...), custom_call_target="tpu_custom_call" | custom-call | flops 20000000000 | bytes 50000000 | tf_op jit(solution)/shard_map/pallas_call | solution.py:484
  456.0 2.4 dynamic-slice_convert_fusion
  464.6 2.2 collective-permute-done.92
  469.2 3.5 collective-permute-done.94
  476.0 10.6 %collective-permute-done.95 = f32[18,384]{1,0:T(8,128)S(1)} collective-permute-done((f32[18,384]{1,0:T(8,128)S(1)}, f32[18,384]{1,0:T(8,128)S(1)}, u32[]{:S(2)}, u32[]{:S(2)}) %collective-permute-start.95) | collective-permute-done | bytes 27680 | tf_op jit(solution)/shard_map/ppermute | solution.py:546
  489.1 4.2 collective-permute-done.65
  493.3 5.8 collective-permute-start.81
  503.7 4.4 collective-permute-done.66
  510.6 5.3 collective-permute-done.62
  516.9 3.7 collective-permute-start.67
  525.4 5.1 collective-permute-start.68
  530.5 3.3 fusion.4
  534.6 3.0 collective-permute-done.53
  543.0 3.4 fusion.2
  550.6 7.4 %collective-permute-done.57 = f32[8,256]{1,0:T(8,128)S(1)} collective-permute-done((f32[8,256]{1,0:T(8,128)S(1)}, f32[8,256]{1,0:T(8,128)S(1)}, u32[]{:S(2)}, u32[]{:S(2)}) %collective-permute-start.57) | collective-permute-done | bytes 8224 | tf_op jit(solution)/shard_map/ppermute | solution.py:546
  559.3 4.6 collective-permute-start.69
  572.4 2.6 collective-permute-start.50
  579.5 7.1 %collective-permute-done.50 = bf16[512,768]{1,0:T(8,128)(2,1)} collective-permute-done((bf16[512,768]{1,0:T(8,128)(2,1)}, bf16[512,768]{1,0:T(8,128)(2,1)}, u32[]{:S(2)}, u32[]{:S(2)}) %collective-permute-start.50) | collective-permute-done | bytes 786464 | tf_op jit(solution)/shard_map/ppermute | solution.py:606
  (477 shorter events, 205.7 us)
Async XLA Ops:
  8.6 65.8 %collective-permute-start.2 = (bf16[96,1024]{1,0:T(8,128)(2,1)}, bf16[96,1024]{1,0:T(8,128)(2,1)}, u32[]{:S(2)}, u32[]{:S(2)}) collective-permute-start(bf16[96,1024]{1,0:T(8,128)(2,1)} %fusion.46), channel_id=1, source_target_pairs={{0,16},{16,0},{1,17},{17,1},{2,18},{18,2},{3,19},{19,3},{4,20},{20... | collective-permute-start | bytes 589832 | tf_op jit(solution)/shard_map/ppermute | solution.py:600
  13.2 48.0 %collective-permute-start.13 = (bf16[96,384]{1,0:T(8,128)(2,1)}, bf16[96,384]{1,0:T(8,128)(2,1)}, u32[]{:S(2)}, u32[]{:S(2)}) collective-permute-start(bf16[96,384]{1,0:T(8,128)(2,1)} %bitcast.400), channel_id=1, source_target_pairs={{0,16},{16,0},{1,17},{17,1},{2,18},{18,2},{3,19},{19,3},{4,20},{20... | collective-permute-start | bytes 221192 | tf_op jit(solution)/shard_map/ppermute | solution.py:600
  15.2 37.2 %collective-permute-start.22 = (f32[6,384]{1,0:T(8,128)}, f32[6,384]{1,0:T(8,128)}, u32[]{:S(2)}, u32[]{:S(2)}) collective-permute-start(f32[6,384]{1,0:T(8,128)} %fusion.54), channel_id=1, source_target_pairs={{0,16},{16,0},{1,17},{17,1},{2,18},{18,2},{3,19},{19,3},{4,20},{20... | collective-permute-start | bytes 27656 | tf_op jit(solution)/shard_map/ppermute | solution.py:600
  17.0 31.2 %collective-permute-start.24 = (f32[8,256]{1,0:T(8,128)}, f32[8,256]{1,0:T(8,128)}, u32[]{:S(2)}, u32[]{:S(2)}) collective-permute-start(f32[8,256]{1,0:T(8,128)} %pad_maximum_fusion.12), channel_id=1, source_target_pairs={{0,16},{16,0},{1,17},{17,1},{2,18},{18,2},{3,19},{19,3},{4,20},{20... | collective-permute-start | bytes 24584 | tf_op jit(solution)/shard_map/ppermute | solution.py:600
  18.9 117.9 %collective-permute-start = (bf16[256,768]{1,0:T(8,128)(2,1)}, bf16[256,768]{1,0:T(8,128)(2,1)}, u32[]{:S(2)}, u32[]{:S(2)}) collective-permute-start(bf16[256,768]{1,0:T(8,128)(2,1)} %dynamic-slice_bitcast_fusion.6), channel_id=1, source_target_pairs={{0,1},{1,0},{2,3},{3,2},{4,5},{5,4},{6,7},{7,6},{8,9},{9,8},{10,11... | collective-permute-start | bytes 1179656 | tf_op jit(solution)/shard_map/ppermute | solution.py:600
  79.8 203.5 %collective-permute-start.45 = (f32[256,768]{1,0:T(8,128)}, f32[256,768]{1,0:T(8,128)}, u32[]{:S(2)}, u32[]{:S(2)}) collective-permute-start(f32[256,768]{1,0:T(8,128)} %dynamic-slice_bitcast_fusion.2), channel_id=1, source_target_pairs={{0,1},{1,0},{2,3},{3,2},{4,5},{5,4},{6,7},{7,6},{8,9},{9,8},{10,11... | collective-permute-start | bytes 2359304 | tf_op jit(solution)/shard_map/ppermute | solution.py:600
  81.6 18.1 %collective-permute-start.40 = (bf16[96,384]{1,0:T(8,128)(2,1)S(1)}, bf16[96,384]{1,0:T(8,128)(2,1)S(1)}, u32[]{:S(2)}, u32[]{:S(2)}) collective-permute-start(bf16[96,384]{1,0:T(8,128)(2,1)S(1)} %collective-permute-done.39), channel_id=1, source_target_pairs={{4,0},{6,2},{8,4},{10,6},{5,1},{7,3},{9,5},{11,7},{20,16},{22,18},... | collective-permute-start | bytes 221192 | tf_op jit(solution)/shard_map/ppermute | solution.py:546
  85.0 29.4 %collective-permute-start.26 = (bf16[96,1024]{1,0:T(8,128)(2,1)S(1)}, bf16[96,1024]{1,0:T(8,128)(2,1)S(1)}, u32[]{:S(2)}, u32[]{:S(2)}) collective-permute-start(bf16[96,1024]{1,0:T(8,128)(2,1)S(1)} %get-tuple-element.192), channel_id=1, source_target_pairs={{0,4},{2,6},{4,8},{6,10},{8,12},{10,14},{1,5},{3,7},{5,9},{7,11},{... | collective-permute-start | bytes 589832 | tf_op jit(solution)/shard_map/ppermute | solution.py:546
  93.3 22.7 %collective-permute-start.3 = (bf16[96,1024]{1,0:T(8,128)(2,1)S(1)}, bf16[96,1024]{1,0:T(8,128)(2,1)S(1)}, u32[]{:S(2)}, u32[]{:S(2)}) collective-permute-start(bf16[96,1024]{1,0:T(8,128)(2,1)S(1)} %get-tuple-element.193), channel_id=1, source_target_pairs={{0,4},{2,6},{4,8},{6,10},{8,12},{10,14},{1,5},{3,7},{5,9},{7,11},{... | collective-permute-start | bytes 589832 | tf_op jit(solution)/shard_map/ppermute | solution.py:546
  121.3 14.2 %collective-permute-start.6 = (bf16[96,1024]{1,0:T(8,128)(2,1)S(1)}, bf16[96,1024]{1,0:T(8,128)(2,1)S(1)}, u32[]{:S(2)}, u32[]{:S(2)}) collective-permute-start(bf16[96,1024]{1,0:T(8,128)(2,1)S(1)} %get-tuple-element.193), channel_id=1, source_target_pairs={{4,0},{6,2},{8,4},{10,6},{12,8},{14,10},{5,1},{7,3},{9,5},{11,7},{... | collective-permute-start | bytes 589832 | tf_op jit(solution)/shard_map/ppermute | solution.py:546
  122.6 15.5 %collective-permute-start.5 = (bf16[96,1024]{1,0:T(8,128)(2,1)S(1)}, bf16[96,1024]{1,0:T(8,128)(2,1)S(1)}, u32[]{:S(2)}, u32[]{:S(2)}) collective-permute-start(bf16[96,1024]{1,0:T(8,128)(2,1)S(1)} %collective-permute-done.4), channel_id=1, source_target_pairs={{8,12},{10,14},{9,13},{11,15},{24,28},{26,30},{25,29},{27,31}} | collective-permute-start | bytes 589832 | tf_op jit(solution)/shard_map/ppermute | solution.py:546
  124.1 95.8 %collective-permute-start.42 = (bf16[4,96,384]{2,1,0:T(8,128)(2,1)}, bf16[4,96,384]{2,1,0:T(8,128)(2,1)}, u32[]{:S(2)}, u32[]{:S(2)}) collective-permute-start(bf16[4,96,384]{2,1,0:T(8,128)(2,1)} %constant_dynamic-slice_fusion.8), channel_id=1, source_target_pairs={{0,2},{2,0},{4,6},{6,4},{8,10},{10,8},{12,14},{14,12},{1,3},{3,1},... | collective-permute-start | bytes 884744 | tf_op jit(solution)/shard_map/ppermute | solution.py:546
  138.1 26.7 %collective-permute-start.1 = (bf16[256,768]{1,0:T(8,128)(2,1)}, bf16[256,768]{1,0:T(8,128)(2,1)S(1)}, u32[]{:S(2)}, u32[]{:S(2)}) collective-permute-start(bf16[256,768]{1,0:T(8,128)(2,1)} %collective-permute-done), channel_id=1, source_target_pairs={{0,16},{16,0},{1,17},{17,1},{2,18},{18,2},{3,19},{19,3},{4,20},{20... | collective-permute-start | bytes 1179656 | tf_op jit(solution)/shard_map/ppermute | solution.py:600
  146.4 43.7 %collective-permute-start.21 = (bf16[768,384]{1,0:T(8,128)(2,1)S(1)}, bf16[768,384]{1,0:T(8,128)(2,1)S(1)}, u32[]{:S(2)}, u32[]{:S(2)}) collective-permute-start(bf16[768,384]{1,0:T(8,128)(2,1)S(1)} %bitcast.444), channel_id=1, source_target_pairs={{0,1},{1,0},{2,3},{3,2},{4,5},{5,4},{6,7},{7,6},{8,9},{9,8},{10,11... | collective-permute-start | bytes 1769480 | tf_op jit(solution)/shard_map/ppermute | solution.py:600
  164.8 12.1 %collective-permute-start.9 = (bf16[4,96,512]{2,1,0:T(8,128)(2,1)S(1)}, bf16[4,96,512]{2,1,0:T(8,128)(2,1)S(1)}, u32[]{:S(2)}, u32[]{:S(2)}) collective-permute-start(bf16[4,96,512]{2,1,0:T(8,128)(2,1)S(1)} %get-tuple-element.175), channel_id=1, source_target_pairs={{0,2},{2,0},{4,6},{6,4},{8,10},{10,8},{12,14},{14,12},{1,3},{3,1},... | collective-permute-start | bytes 1179656 | tf_op jit(solution)/shard_map/ppermute | solution.py:546
  174.1 12.8 %collective-permute-start.12 = (bf16[2,4,96,512]{3,2,1,0:T(8,128)(2,1)S(1)}, bf16[2,4,96,512]{3,2,1,0:T(8,128)(2,1)S(1)}, u32[]{:S(2)}, u32[]{:S(2)}) collective-permute-start(bf16[2,4,96,512]{3,2,1,0:T(8,128)(2,1)S(1)} %pad_maximum_fusion.2), channel_id=1, source_target_pairs={{0,2},{2,0},{4,6},{6,4},{8,10},{10,8},{12,14},{14,12},{1,3},{3,1},... | collective-permute-start | bytes 2359304 | tf_op jit(solution)/shard_map/ppermute | solution.py:546
  177.1 16.3 %collective-permute-start.10 = (bf16[768,512]{1,0:T(8,128)(2,1)S(1)}, bf16[768,512]{1,0:T(8,128)(2,1)S(1)}, u32[]{:S(2)}, u32[]{:S(2)}) collective-permute-start(bf16[768,512]{1,0:T(8,128)(2,1)S(1)} %bitcast.433), channel_id=1, source_target_pairs={{0,1},{1,0},{2,3},{3,2},{4,5},{5,4},{6,7},{7,6},{8,9},{9,8},{10,11... | collective-permute-start | bytes 2359304 | tf_op jit(solution)/shard_map/ppermute | solution.py:600
  186.9 30.3 %collective-permute-start.34 = (bf16[4,96,512]{2,1,0:T(8,128)(2,1)S(1)}, bf16[4,96,512]{2,1,0:T(8,128)(2,1)}, u32[]{:S(2)}, u32[]{:S(2)}) collective-permute-start(bf16[4,96,512]{2,1,0:T(8,128)(2,1)S(1)} %get-tuple-element.172), channel_id=1, source_target_pairs={{0,1},{1,0},{2,3},{3,2},{4,5},{5,4},{6,7},{7,6},{8,9},{9,8},{10,11... | collective-permute-start | bytes 1179656 | tf_op jit(solution)/shard_map/ppermute | solution.py:600
  215.3 44.7 %collective-permute-start.25 = (bf16[1024,896]{1,0:T(8,128)(2,1)}, bf16[1024,896]{1,0:T(8,128)(2,1)}, u32[]{:S(2)}, u32[]{:S(2)}) collective-permute-start(bf16[1024,896]{1,0:T(8,128)(2,1)} %get-tuple-element.53.refs_1_), channel_id=1, source_target_pairs={{0,16},{16,0},{1,17},{17,1},{2,18},{18,2},{3,19},{19,3},{4,20},{20... | collective-permute-start | bytes 5505032 | tf_op jit(solution)/shard_map/ppermute | solution.py:600
  215.5 11.9 %collective-permute-start.32 = (bf16[4,96,512]{2,1,0:T(8,128)(2,1)S(1)}, bf16[4,96,512]{2,1,0:T(8,128)(2,1)S(1)}, u32[]{:S(2)}, u32[]{:S(2)}) collective-permute-start(bf16[4,96,512]{2,1,0:T(8,128)(2,1)S(1)} %get-tuple-element.173), channel_id=1, source_target_pairs={{0,2},{2,0},{4,6},{6,4},{8,10},{10,8},{12,14},{14,12},{1,3},{3,1},... | collective-permute-start | bytes 1179656 | tf_op jit(solution)/shard_map/ppermute | solution.py:546
  218.3 25.6 %collective-permute-start.35 = (bf16[2,4,96,512]{3,2,1,0:T(8,128)(2,1)S(1)}, bf16[2,4,96,512]{3,2,1,0:T(8,128)(2,1)S(1)}, u32[]{:S(2)}, u32[]{:S(2)}) collective-permute-start(bf16[2,4,96,512]{3,2,1,0:T(8,128)(2,1)S(1)} %pad_maximum_fusion.3), channel_id=1, source_target_pairs={{0,2},{2,0},{4,6},{6,4},{8,10},{10,8},{12,14},{14,12},{1,3},{3,1},... | collective-permute-start | bytes 2359304 | tf_op jit(solution)/shard_map/ppermute | solution.py:546
  227.6 31.4 %collective-permute-start.33 = (bf16[768,512]{1,0:T(8,128)(2,1)S(1)}, bf16[768,512]{1,0:T(8,128)(2,1)S(1)}, u32[]{:S(2)}, u32[]{:S(2)}) collective-permute-start(bf16[768,512]{1,0:T(8,128)(2,1)S(1)} %bitcast.436), channel_id=1, source_target_pairs={{0,1},{1,0},{2,3},{3,2},{4,5},{5,4},{6,7},{7,6},{8,9},{9,8},{10,11... | collective-permute-start | bytes 2359304 | tf_op jit(solution)/shard_map/ppermute | solution.py:600
  229.2 29.8 %collective-permute-start.43 = (bf16[768,384]{1,0:T(8,128)(2,1)S(1)}, bf16[768,384]{1,0:T(8,128)(2,1)S(1)}, u32[]{:S(2)}, u32[]{:S(2)}) collective-permute-start(bf16[768,384]{1,0:T(8,128)(2,1)S(1)} %bitcast.447), channel_id=1, source_target_pairs={{0,1},{1,0},{2,3},{3,2},{4,5},{5,4},{6,7},{7,6},{8,9},{9,8},{10,11... | collective-permute-start | bytes 1769480 | tf_op jit(solution)/shard_map/ppermute | solution.py:600
  337.0 36.4 %collective-permute-start.73 = (bf16[768,512]{1,0:T(8,128)(2,1)}, bf16[768,512]{1,0:T(8,128)(2,1)}, u32[]{:S(2)}, u32[]{:S(2)}) collective-permute-start(bf16[768,512]{1,0:T(8,128)(2,1)} %get-tuple-element.87), channel_id=1, source_target_pairs={{0,1},{1,0},{2,3},{3,2},{4,5},{5,4},{6,7},{7,6},{8,9},{9,8},{10,11... | collective-permute-start | bytes 2359304 | tf_op jit(solution)/shard_map/ppermute | solution.py:600
  339.7 35.7 %collective-permute-start.75 = (bf16[2,4,96,512]{3,2,1,0:T(8,128)(2,1)S(1)}, bf16[2,4,96,512]{3,2,1,0:T(8,128)(2,1)}, u32[]{:S(2)}, u32[]{:S(2)}) collective-permute-start(bf16[2,4,96,512]{3,2,1,0:T(8,128)(2,1)S(1)} %fusion.9), channel_id=1, source_target_pairs={{0,2},{2,0},{4,6},{6,4},{8,10},{10,8},{12,14},{14,12},{1,3},{3,1},... | collective-permute-start | bytes 2359304 | tf_op jit(solution)/shard_map/ppermute | solution.py:546
  340.3 30.1 %collective-permute-start.77 = (bf16[768,384]{1,0:T(8,128)(2,1)}, bf16[768,384]{1,0:T(8,128)(2,1)}, u32[]{:S(2)}, u32[]{:S(2)}) collective-permute-start(bf16[768,384]{1,0:T(8,128)(2,1)} %get-tuple-element.91), channel_id=1, source_target_pairs={{0,1},{1,0},{2,3},{3,2},{4,5},{5,4},{6,7},{7,6},{8,9},{9,8},{10,11... | collective-permute-start | bytes 1769480 | tf_op jit(solution)/shard_map/ppermute | solution.py:600
  342.0 56.7 %collective-permute-start.48 = (bf16[1024,768]{1,0:T(8,128)(2,1)}, bf16[1024,768]{1,0:T(8,128)(2,1)}, u32[]{:S(2)}, u32[]{:S(2)}) collective-permute-start(bf16[1024,768]{1,0:T(8,128)(2,1)} %get-tuple-element.66.refs_5_), channel_id=1, source_target_pairs={{0,16},{16,0},{1,17},{17,1},{2,18},{18,2},{3,19},{19,3},{4,20},{20... | collective-permute-start | bytes 4718600 | tf_op jit(solution)/shard_map/ppermute | solution.py:600
  344.2 42.9 %collective-permute-start.47 = (bf16[512,768]{1,0:T(8,128)(2,1)S(1)}, bf16[512,768]{1,0:T(8,128)(2,1)S(1)}, u32[]{:S(2)}, u32[]{:S(2)}) collective-permute-start(bf16[512,768]{1,0:T(8,128)(2,1)S(1)} %get-tuple-element.161), channel_id=1, source_target_pairs={{0,1},{1,0},{2,3},{3,2},{4,5},{5,4},{6,7},{7,6},{8,9},{9,8},{10,11... | collective-permute-start | bytes 2359304 | tf_op jit(solution)/shard_map/ppermute | solution.py:600
  371.7 16.9 %collective-permute-start.78 = (bf16[1,4,96,384]{3,2,1,0:T(8,128)(2,1)S(1)}, bf16[1,4,96,384]{3,2,1,0:T(8,128)(2,1)S(1)}, u32[]{:S(2)}, u32[]{:S(2)}) collective-permute-start(bf16[1,4,96,384]{3,2,1,0:T(8,128)(2,1)S(1)} %dynamic-slice_bitcast_fusion.7), channel_id=1, source_target_pairs={{0,2},{2,0},{4,6},{6,4},{8,10},{10,8},{12,14},{14,12},{1,3},{3,1},... | collective-permute-start | bytes 884744 | tf_op jit(solution)/shard_map/ppermute | solution.py:546
  374.9 13.7 %collective-permute-start.74 = (bf16[1,4,96,512]{3,2,1,0:T(8,128)(2,1)S(1)}, bf16[1,4,96,512]{3,2,1,0:T(8,128)(2,1)S(1)}, u32[]{:S(2)}, u32[]{:S(2)}) collective-permute-start(bf16[1,4,96,512]{3,2,1,0:T(8,128)(2,1)S(1)} %dynamic-slice_bitcast_fusion.4), channel_id=1, source_target_pairs={{0,2},{2,0},{4,6},{6,4},{8,10},{10,8},{12,14},{14,12},{1,3},{3,1},... | collective-permute-start | bytes 1179656 | tf_op jit(solution)/shard_map/ppermute | solution.py:546
  376.8 18.0 %collective-permute-start.76 = (bf16[4,96,512]{2,1,0:T(8,128)(2,1)S(1)}, bf16[4,96,512]{2,1,0:T(8,128)(2,1)S(1)}, u32[]{:S(2)}, u32[]{:S(2)}) collective-permute-start(bf16[4,96,512]{2,1,0:T(8,128)(2,1)S(1)} %slice_bitcast_fusion), channel_id=1, source_target_pairs={{0,1},{1,0},{2,3},{3,2},{4,5},{5,4},{6,7},{7,6},{8,9},{9,8},{10,11... | collective-permute-start | bytes 1179656 | tf_op jit(solution)/shard_map/ppermute | solution.py:600
  395.1 51.2 %collective-permute-start.79 = (bf16[96,1408]{1,0:T(8,128)(2,1)S(1)}, bf16[96,1408]{1,0:T(8,128)(2,1)}, u32[]{:S(2)}, u32[]{:S(2)}) collective-permute-start(bf16[96,1408]{1,0:T(8,128)(2,1)S(1)} %get-tuple-element.178), channel_id=1, source_target_pairs={{0,4},{2,6},{1,5},{3,7},{16,20},{18,22},{17,21},{19,23}} | collective-permute-start | bytes 811016 | tf_op jit(solution)/shard_map/ppermute | solution.py:546
  397.3 76.1 %collective-permute-start.82 = (bf16[96,1408]{1,0:T(8,128)(2,1)S(1)}, bf16[96,1408]{1,0:T(8,128)(2,1)}, u32[]{:S(2)}, u32[]{:S(2)}) collective-permute-start(bf16[96,1408]{1,0:T(8,128)(2,1)S(1)} %get-tuple-element.179), channel_id=1, source_target_pairs={{12,8},{14,10},{13,9},{15,11},{28,24},{30,26},{29,25},{31,27}} | collective-permute-start | bytes 811016 | tf_op jit(solution)/shard_map/ppermute | solution.py:546
  448.0 25.5 %collective-permute-start.80 = (bf16[96,1408]{1,0:T(8,128)(2,1)}, bf16[96,1408]{1,0:T(8,128)(2,1)S(1)}, u32[]{:S(2)}, u32[]{:S(2)}) collective-permute-start(bf16[96,1408]{1,0:T(8,128)(2,1)} %fusion.24), channel_id=1, source_target_pairs={{0,4},{2,6},{4,8},{6,10},{1,5},{3,7},{5,9},{7,11},{16,20},{18,22},... | collective-permute-start | bytes 811016 | tf_op jit(solution)/shard_map/ppermute | solution.py:546
  462.8 39.1 %collective-permute-start.61 = (bf16[768,512]{1,0:T(8,128)(2,1)}, bf16[768,512]{1,0:T(8,128)(2,1)}, u32[]{:S(2)}, u32[]{:S(2)}) collective-permute-start(bf16[768,512]{1,0:T(8,128)(2,1)} %get-tuple-element.81), channel_id=1, source_target_pairs={{0,1},{1,0},{2,3},{3,2},{4,5},{5,4},{6,7},{7,6},{8,9},{9,8},{10,11... | collective-permute-start | bytes 2359304 | tf_op jit(solution)/shard_map/ppermute | solution.py:600
  468.2 32.2 %collective-permute-start.63 = (bf16[2,4,96,512]{3,2,1,0:T(8,128)(2,1)}, bf16[2,4,96,512]{3,2,1,0:T(8,128)(2,1)S(1)}, u32[]{:S(2)}, u32[]{:S(2)}) collective-permute-start(bf16[2,4,96,512]{3,2,1,0:T(8,128)(2,1)} %fusion.13), channel_id=1, source_target_pairs={{0,2},{2,0},{4,6},{6,4},{8,10},{10,8},{12,14},{14,12},{1,3},{3,1},... | collective-permute-start | bytes 2359304 | tf_op jit(solution)/shard_map/ppermute | solution.py:546
  472.7 20.6 %collective-permute-start.65 = (bf16[768,384]{1,0:T(8,128)(2,1)}, bf16[768,384]{1,0:T(8,128)(2,1)S(1)}, u32[]{:S(2)}, u32[]{:S(2)}) collective-permute-start(bf16[768,384]{1,0:T(8,128)(2,1)} %get-tuple-element.85), channel_id=1, source_target_pairs={{0,1},{1,0},{2,3},{3,2},{4,5},{5,4},{6,7},{7,6},{8,9},{9,8},{10,11... | collective-permute-start | bytes 1769480 | tf_op jit(solution)/shard_map/ppermute | solution.py:600
  473.4 57.0 %collective-permute-start.49 = (bf16[1024,768]{1,0:T(8,128)(2,1)}, bf16[1024,768]{1,0:T(8,128)(2,1)S(1)}, u32[]{:S(2)}, u32[]{:S(2)}) collective-permute-start(bf16[1024,768]{1,0:T(8,128)(2,1)} %get-tuple-element.76), channel_id=1, source_target_pairs={{0,16},{16,0},{1,17},{17,1},{2,18},{18,2},{3,19},{19,3},{4,20},{20... | collective-permute-start | bytes 4718600 | tf_op jit(solution)/shard_map/ppermute | solution.py:600
  473.5 13.1 %collective-permute-start.95 = (f32[18,384]{1,0:T(8,128)S(1)}, f32[18,384]{1,0:T(8,128)S(1)}, u32[]{:S(2)}, u32[]{:S(2)}) collective-permute-start(f32[18,384]{1,0:T(8,128)S(1)} %add_add_fusion), channel_id=1, source_target_pairs={{0,2},{2,0},{4,6},{6,4},{8,10},{10,8},{12,14},{14,12},{1,3},{3,1},... | collective-permute-start | bytes 82952 | tf_op jit(solution)/shard_map/ppermute | solution.py:546
  486.6 34.1 %collective-permute-start.83 = (bf16[96,1408]{1,0:T(8,128)(2,1)S(1)}, bf16[96,1408]{1,0:T(8,128)(2,1)S(1)}, u32[]{:S(2)}, u32[]{:S(2)}) collective-permute-start(bf16[96,1408]{1,0:T(8,128)(2,1)S(1)} %get-tuple-element.177), channel_id=1, source_target_pairs={{8,4},{10,6},{12,8},{14,10},{9,5},{11,7},{13,9},{15,11},{24,20},{2... | collective-permute-start | bytes 811016 | tf_op jit(solution)/shard_map/ppermute | solution.py:546
  493.3 79.1 %collective-permute-start.81 = (bf16[96,1408]{1,0:T(8,128)(2,1)}, bf16[96,1408]{1,0:T(8,128)(2,1)S(1)}, u32[]{:S(2)}, u32[]{:S(2)}) collective-permute-start(bf16[96,1408]{1,0:T(8,128)(2,1)} %get-tuple-element.176), channel_id=1, source_target_pairs={{0,4},{2,6},{4,8},{6,10},{8,12},{10,14},{1,5},{3,7},{5,9},{7,11},{... | collective-permute-start | bytes 811016 | tf_op jit(solution)/shard_map/ppermute | solution.py:546
  521.4 53.6 %collective-permute-start.84 = (bf16[96,1408]{1,0:T(8,128)(2,1)}, bf16[96,1408]{1,0:T(8,128)(2,1)S(1)}, u32[]{:S(2)}, u32[]{:S(2)}) collective-permute-start(bf16[96,1408]{1,0:T(8,128)(2,1)} %fusion.23), channel_id=1, source_target_pairs={{4,0},{6,2},{8,4},{10,6},{12,8},{14,10},{5,1},{7,3},{9,5},{11,7},{... | collective-permute-start | bytes 811016 | tf_op jit(solution)/shard_map/ppermute | solution.py:546
  522.7 16.1 %collective-permute-start.70 = (bf16[96,1408]{1,0:T(8,128)(2,1)}, bf16[96,1408]{1,0:T(8,128)(2,1)}, u32[]{:S(2)}, u32[]{:S(2)}) collective-permute-start(bf16[96,1408]{1,0:T(8,128)(2,1)} %get-tuple-element.183), channel_id=1, source_target_pairs={{12,8},{14,10},{13,9},{15,11},{28,24},{30,26},{29,25},{31,27}} | collective-permute-start | bytes 811016 | tf_op jit(solution)/shard_map/ppermute | solution.py:546
  525.4 14.8 %collective-permute-start.68 = (bf16[96,1408]{1,0:T(8,128)(2,1)}, bf16[96,1408]{1,0:T(8,128)(2,1)}, u32[]{:S(2)}, u32[]{:S(2)}) collective-permute-start(bf16[96,1408]{1,0:T(8,128)(2,1)} %fusion.30), channel_id=1, source_target_pairs={{0,4},{2,6},{4,8},{6,10},{1,5},{3,7},{5,9},{7,11},{16,20},{18,22},... | collective-permute-start | bytes 811016 | tf_op jit(solution)/shard_map/ppermute | solution.py:546
  542.2 17.1 %collective-permute-start.71 = (bf16[96,1408]{1,0:T(8,128)(2,1)S(1)}, bf16[96,1408]{1,0:T(8,128)(2,1)S(1)}, u32[]{:S(2)}, u32[]{:S(2)}) collective-permute-start(bf16[96,1408]{1,0:T(8,128)(2,1)S(1)} %get-tuple-element.181), channel_id=1, source_target_pairs={{8,4},{10,6},{12,8},{14,10},{9,5},{11,7},{13,9},{15,11},{24,20},{2... | collective-permute-start | bytes 811016 | tf_op jit(solution)/shard_map/ppermute | solution.py:546
  550.0 14.7 %collective-permute-start.58 = (f32[8,256]{1,0:T(8,128)S(1)}, f32[8,256]{1,0:T(8,128)S(1)}, u32[]{:S(2)}, u32[]{:S(2)}) collective-permute-start(f32[8,256]{1,0:T(8,128)S(1)} %collective-permute-done.56), channel_id=1, source_target_pairs={{8,12},{10,14},{9,13},{11,15},{24,28},{26,30},{25,29},{27,31}} | collective-permute-start | bytes 24584 | tf_op jit(solution)/shard_map/ppermute | solution.py:546
  559.3 15.7 %collective-permute-start.69 = (bf16[96,1408]{1,0:T(8,128)(2,1)}, bf16[96,1408]{1,0:T(8,128)(2,1)S(1)}, u32[]{:S(2)}, u32[]{:S(2)}) collective-permute-start(bf16[96,1408]{1,0:T(8,128)(2,1)} %get-tuple-element.180), channel_id=1, source_target_pairs={{0,4},{2,6},{4,8},{6,10},{8,12},{10,14},{1,5},{3,7},{5,9},{7,11},{... | collective-permute-start | bytes 811016 | tf_op jit(solution)/shard_map/ppermute | solution.py:546
  572.4 14.2 %collective-permute-start.50 = (bf16[512,768]{1,0:T(8,128)(2,1)}, bf16[512,768]{1,0:T(8,128)(2,1)}, u32[]{:S(2)}, u32[]{:S(2)}) collective-permute-start(bf16[512,768]{1,0:T(8,128)(2,1)} %dynamic-slice_convert_fusion.1), channel_id=1, source_target_pairs={{0,1},{1,0},{2,3},{3,2},{4,5},{5,4},{6,7},{7,6},{8,9},{9,8},{10,11... | collective-permute-start | bytes 2359304 | tf_op jit(solution)/shard_map/ppermute | solution.py:606
  (94 other events, 749.0 us)
